TPU v7x, 512 devices: a whole 4x4x16 slice. The times are simulated.
512 devices in a mesh: cin: 16 (over z), cout: 8 (over y, core), sp: 4 (over x).
Axes of the slice: x: 4, y: 4, z: 16, core: 2. Of those that a mesh axis runs over, the one named last changes fastest.
Arguments:
- activations: bfloat16 [512, 4, 32, 128], P('cin', 'sp', 'cout'), may hold values from -6 to 6
- weights: bfloat16 [3, 3, 3, 512, 512], P(None, None, None, 'cin', 'cout'), may hold values from -0.0546875 to 0.0546875
- out_grad: bfloat16 [512, 4, 32, 128], P('cout', 'sp', 'cin'), may hold values from -6 to 6
Outputs:
- output: bfloat16 [512, 4, 32, 128], P('cout', 'sp', 'cin')
- in_grad: bfloat16 [512, 4, 32, 128], P('cin', 'sp', 'cout')
- weight_grad: bfloat16 [3, 3, 3, 512, 512], P(None, None, None, 'cin', 'cout')
All inputs are finite; a program needn't handle non-finite values.
Results may differ from a plain program's by a relative error of at most 0.001.
Values may be sent and summed in bfloat16 or wider, within the bound.
No kernel may reach another device: no remote copies, remote signals or barrier semaphores. Data moves between devices by JAX's collectives and lax.ppermute only.
A program may use at most 64 MiB of HBM per device.

v0:
```python
import math

import jax
import jax.numpy as jnp
from jax import lax
from jax.sharding import PartitionSpec as P


def with_halo(block, sides, width):
    for axis, dim in sides:
        count = lax.axis_size(axis)
        forward = [(i, i + 1) for i in range(count - 1)]
        backward = [(target, source) for source, target in forward]
        low = lax.ppermute(
            lax.slice_in_dim(block, block.shape[dim] - width, None, axis=dim), axis, forward
        )
        high = lax.ppermute(lax.slice_in_dim(block, 0, width, axis=dim), axis, backward)
        block = jnp.concatenate([low, block, high], axis=dim)
    return block


def convolve(field, kernel, padding):
    return lax.conv_general_dilated(
        field[None],
        kernel,
        (1, 1, 1),
        padding,
        dimension_numbers=("NCDHW", "DHWIO", "NCDHW"),
        preferred_element_type=jnp.float32,
    )[0]


def body(activations, weights, out_grad):
    x_panel = lax.all_gather(activations, "cout", axis=2, tiled=True)
    x_halo = with_halo(x_panel, (("sp", 1),), 1)
    g_panel = lax.all_gather(out_grad, "cin", axis=2, tiled=True)
    g_halo = with_halo(g_panel, (("sp", 1),), 1)
    partial_out = convolve(x_halo, weights, [(0, 0), (1, 1), (1, 1)])
    output = lax.psum_scatter(partial_out, "cin", scatter_dimension=2, tiled=True).astype(
        jnp.bfloat16
    )
    flipped = jnp.transpose(weights[::-1, ::-1, ::-1], (0, 1, 2, 4, 3))
    dx_partial = convolve(g_halo, flipped, [(0, 0), (1, 1), (1, 1)])
    in_grad = lax.psum_scatter(dx_partial, "cout", scatter_dimension=2, tiled=True).astype(
        jnp.bfloat16
    )
    g_inner = g_halo[:, 1:-1]
    slab_depth = g_inner.shape[1]
    rows_full = g_inner.shape[2]
    row_length = g_inner.shape[3]
    padded = jnp.pad(x_halo, ((0, 0), (0, 0), (1, 1), (1, 1)))
    tap_terms = []
    for a in range(3):
        for b in range(3):
            for c in range(3):
                window = padded[:, a : a + slab_depth, b : b + rows_full, c : c + row_length]
                tap_terms.append(
                    jnp.einsum("cdhw,odhw->co", window, g_inner, preferred_element_type=jnp.float32)
                )
    local_grad = jnp.stack(tap_terms).reshape(3, 3, 3, weights.shape[3], weights.shape[4])
    summed = lax.psum(local_grad, "sp")
    grad_scale = 1.0 / math.sqrt(slab_depth * lax.axis_size("sp") * rows_full * row_length)
    weight_grad = (summed * grad_scale).astype(jnp.bfloat16)
    return (output, in_grad, weight_grad)


def solution(mesh):
    placed = (
        P("cin", "sp", "cout", None),
        P(None, None, None, "cin", "cout"),
        P("cout", "sp", "cin", None),
    )
    return jax.shard_map(
        body,
        mesh=mesh,
        in_specs=placed,
        out_specs=(
            P("cout", "sp", "cin", None),
            P("cin", "sp", "cout", None),
            P(None, None, None, "cin", "cout"),
        ),
        check_vma=False,
    )
```

profile of v0, /device:TPU:24, one launch (start us, length us, event | category | flops | bytes accessed | tf_op | source)
XLA Modules:
  0.0 240.6 jit_solution(12239247400781158167)
XLA Ops:
  8.1 0.8 copy.39
  8.9 15.2 %all_gather.6 = bf16[32,1,32,128]{3,0,1,2:T(8,128)(2,1)S(1)} all-gather(bf16[32,1,4,128]{3,0,1,2:T(8,128)(2,1)S(1)} %copy.39), channel_id=1, replica_groups=mesh['cin'=16,'cout'=8,'sp'=4] {'cout'}, dimensions={2}, use_global_device_ids=true | all-gather | bytes 294912 | tf_op jit(solution)/shard_map/all_gather | solution.py:34
  24.1 1.3 collective-permute-start
  25.4 1.3 collective-permute-start.1
  26.7 0.8 copy.48
  27.5 38.0 %all_gather.7 = bf16[64,1,32,128]{3,0,1,2:T(8,128)(2,1)S(1)} all-gather(bf16[64,1,2,128]{3,0,1,2:T(8,128)(2,1)S(1)} %copy.48), channel_id=1, replica_groups=mesh['cin'=16,'cout'=8,'sp'=4] {'cin'}, dimensions={2}, use_global_device_ids=true | all-gather | bytes 557056 | tf_op jit(solution)/shard_map/all_gather | solution.py:36
  65.5 1.2 copy.49
  66.7 5.6 %collective-permute-start.2 = (bf16[64,1,32,128]{3,2,1,0:T(8,128)(2,1)}, bf16[64,1,32,128]{3,2,1,0:T(8,128)(2,1)}, u32[]{:S(2)}, u32[]{:S(2)}) collective-permute-start(bf16[64,1,32,128]{3,2,1,0:T(8,128)(2,1)} %copy.49), channel_id=1, source_target_pairs={{0,1},{1,2},{2,3},{4,5},{5,6},{6,7},{8,9},{9,10},{10,11},{12,13},{... | collective-permute-start | bytes 1572872 | tf_op jit(solution)/shard_map/ppermute | solution.py:14
  72.3 1.3 collective-permute-start.3
  73.6 2.5 %copy.52 = bf16[64,1,32,128]{0,2,3,1:T(8,128)(2,1)} copy(bf16[64,1,32,128]{3,0,1,2:T(8,128)(2,1)S(1)} %all_gather.7) | data formatting | bytes 1048576 | tf_op jit(solution)/shard_map/all_gather | solution.py:36
  76.1 1.0 pad_maximum_fusion
  78.0 0.3 fusion.47
  78.6 0.3 fusion.45
  78.9 0.3 fusion.44
  79.5 0.3 fusion.42
  79.8 0.3 fusion.41
  80.8 0.3 fusion.38
  81.3 0.3 fusion.36
  81.7 0.3 fusion.35
  82.3 0.3 fusion.33
  82.6 0.3 fusion.32
  83.5 0.3 fusion.29
  84.1 0.3 fusion.27
  84.5 0.3 fusion.26
  85.4 0.8 copy-done.2
  86.2 6.2 %copy.60 = bf16[32,3,32,1,128]{2,0,4,1,3:T(8,128)(2,1)S(1)} copy(bf16[32,3,32,1,128]{4,0,2,1,3:T(8,128)(2,1)} %get-tuple-element.13) | data formatting | bytes 1572864
  92.5 2.4 %pad.5.clone = bf16[32,3,32,1,136]{2,0,4,1,3:T(8,128)(2,1)} pad(bf16[32,3,32,1,128]{2,0,4,1,3:T(8,128)(2,1)S(1)} %copy.60, bf16[]{:T(256)} %constant.1.clone.1), padding=0_0x0_0x0_0x0_0x1_7 | pad | bytes 1622018 | tf_op jit(solution)/shard_map/broadcast_in_dim | solution.py:24
  94.9 7.5 %copy.45 = bf16[32,3,32,1,8,17]{0,4,5,2,1,3:T(8,128)(2,1)} copy(bf16[32,3,32,1,8,17]{2,0,5,4,1,3:T(8,128)(2,1)} %bitcast.304) | data formatting | bytes 1671168 | tf_op jit(solution)/shard_map/conv_general_dilated | solution.py:23
  102.4 1.9 slice.106
  104.4 2.8 %copy.51 = bf16[64,1,32,128]{0,2,3,1:T(8,128)(2,1)S(1)} copy(bf16[64,1,32,128]{3,2,1,0:T(8,128)(2,1)} %collective-permute-done.2) | data formatting | bytes 1048576 | tf_op jit(solution)/shard_map/ppermute | solution.py:14
  107.2 2.8 %copy.53 = bf16[64,1,32,128]{0,2,3,1:T(8,128)(2,1)S(1)} copy(bf16[64,1,32,128]{3,2,1,0:T(8,128)(2,1)} %collective-permute-done.3) | data formatting | bytes 1048576 | tf_op jit(solution)/shard_map/ppermute | solution.py:17
  110.0 0.8 maximum_bitcast_fusion
  110.8 0.7 pad.7
  111.6 1.3 copy.55
  113.0 8.9 %fusion.21 = f32[1,32,8,17,32]{4,2,3,1,0:T(8,128)S(1)} fusion(bf16[3,3,3,32,64]{4,3,2,1,0:T(8,128)(2,1)S(1)} %copy-done, bf16[64,3,32,1,7,2]{0,4,5,2,1,3:T(8,128)(2,1)S(1)} %slice.108, bf16[64,3,32,1,8,17]{0,4,5,2,1,3:T(8,128)(2,1)S(1)} %copy.55, pred[8,17]{0,1:T(8,128)(4,1)S(1)} %copy-done.4), kind=kOutput, calls=%fused_computation.46 | convolution fusion | flops 477011968 | bytes 2510984 | tf_op jit(solution)/shard_map/conv_general_dilated | solution.py:23
  121.9 0.4 copy.56
  122.5 2.1 copy.57
  124.7 5.9 %fusion.18 = f32[1,32,8,17,64]{4,2,3,1,0:T(8,128)S(1)} fusion(bf16[3,3,3,32,64]{4,3,2,1,0:T(8,128)(2,1)S(1)} %copy-done, bf16[32,3,32,1,7,2]{0,4,5,2,1,3:T(8,128)(2,1)S(1)} %copy-done.3, bf16[32,3,32,1,8,17]{0,4,5,2,1,3:T(8,128)(2,1)} %copy.45, pred[8,17]{0,1:T(8,128)(4,1)S(1)} %copy-done.4), kind=kOutput, calls=%fused_computation.45 | convolution fusion | flops 474349568 | bytes 2146440 | tf_op jit(solution)/shard_map/conv_general_dilated | solution.py:23
  130.6 0.4 copy.46
  131.2 2.3 copy.47
  133.5 6.9 %all-reduce.3.cloned.1.call-done = f32[3,3,3,32,64]{4,3,2,1,0:T(8,128)} async-done(((f32[3,3,3,32,64]{4,3,2,1,0:T(8,128)}), f32[3,3,3,32,64]{4,3,2,1,0:T(8,128)}) %all-reduce.3.cloned.1.call-update) | async-done | bytes 221200 | tf_op jit(solution)/shard_map/psum | solution.py:61
  140.3 1.7 multiply_convert_fusion
  142.1 14.2 %reduce-scatter.5.cloned.1.call-done = f32[32,1,4,128]{3,0,1,2:T(8,128)} async-done(((f32[32,1,32,128]{3,0,1,2:T(8,128)}), f32[32,1,4,128]{3,0,1,2:T(8,128)}) %reduce-scatter.5.cloned.1.call-update) | async-done | bytes 65552 | tf_op jit(solution)/shard_map/reduce_scatter | solution.py:44
  156.3 0.8 convert_element_type.12
  157.2 0.6 copy.59
  157.8 73.9 %reduce-scatter.3.cloned.1.call-done = f32[64,1,2,128]{3,0,1,2:T(8,128)} async-done(((f32[64,1,32,128]{3,0,1,2:T(8,128)}), f32[64,1,2,128]{3,0,1,2:T(8,128)}) %reduce-scatter.3.cloned.1.call-update) | async-done | bytes 65552 | tf_op jit(solution)/shard_map/reduce_scatter | solution.py:39
  231.7 0.8 convert_element_type.11
  232.5 0.6 copy.58
  (36 shorter events, 4.7 us)
Async XLA Ops:
  8.0 105.0 %copy-start = (bf16[3,3,3,32,64]{4,3,2,1,0:T(8,128)(2,1)S(1)}, bf16[3,3,3,32,64]{4,3,2,1,0:T(8,128)(2,1)}, u32[]{:S(2)}) copy-start(bf16[3,3,3,32,64]{4,3,2,1,0:T(8,128)(2,1)} %param.4) | copy-start | bytes 331780
  8.0 132.3 %all-reduce.3.cloned.1.call-start = ((), (), s32[]{:S(2)}) async-start(), calls=%async_computation.4 | async-start | bytes 884736 | tf_op jit(solution)/shard_map/psum | solution.py:61
  24.1 52.0 %collective-permute-start = (bf16[32,1,32,128]{3,0,2,1:T(8,128)(2,1)S(1)}, bf16[32,1,32,128]{3,0,2,1:T(8,128)(2,1)S(1)}, u32[]{:S(2)}, u32[]{:S(2)}) collective-permute-start(bf16[32,1,32,128]{3,0,2,1:T(8,128)(2,1)S(1)} %bitcast.307), channel_id=1, source_target_pairs={{0,1},{1,2},{2,3},{4,5},{5,6},{6,7},{8,9},{9,10},{10,11},{12,13},{... | collective-permute-start | bytes 786440 | tf_op jit(solution)/shard_map/ppermute | solution.py:14
  25.4 50.7 %collective-permute-start.1 = (bf16[32,1,32,128]{3,0,2,1:T(8,128)(2,1)S(1)}, bf16[32,1,32,128]{3,0,2,1:T(8,128)(2,1)S(1)}, u32[]{:S(2)}, u32[]{:S(2)}) collective-permute-start(bf16[32,1,32,128]{3,0,2,1:T(8,128)(2,1)S(1)} %bitcast.308), channel_id=1, source_target_pairs={{1,0},{2,1},{3,2},{5,4},{6,5},{7,6},{9,8},{10,9},{11,10},{13,12},{... | collective-permute-start | bytes 786440 | tf_op jit(solution)/shard_map/ppermute | solution.py:17
  66.7 37.7 %collective-permute-start.2 = (bf16[64,1,32,128]{3,2,1,0:T(8,128)(2,1)}, bf16[64,1,32,128]{3,2,1,0:T(8,128)(2,1)}, u32[]{:S(2)}, u32[]{:S(2)}) collective-permute-start(bf16[64,1,32,128]{3,2,1,0:T(8,128)(2,1)} %copy.49), channel_id=1, source_target_pairs={{0,1},{1,2},{2,3},{4,5},{5,6},{6,7},{8,9},{9,10},{10,11},{12,13},{... | collective-permute-start | bytes 1572872 | tf_op jit(solution)/shard_map/ppermute | solution.py:14
  72.3 34.9 %collective-permute-start.3 = (bf16[64,1,32,128]{3,2,1,0:T(8,128)(2,1)}, bf16[64,1,32,128]{3,2,1,0:T(8,128)(2,1)}, u32[]{:S(2)}, u32[]{:S(2)}) collective-permute-start(bf16[64,1,32,128]{3,2,1,0:T(8,128)(2,1)} %copy.49), channel_id=1, source_target_pairs={{1,0},{2,1},{3,2},{5,4},{6,5},{7,6},{9,8},{10,9},{11,10},{13,12},{... | collective-permute-start | bytes 1572872 | tf_op jit(solution)/shard_map/ppermute | solution.py:17
  85.4 0.8 copy-start.2
  86.2 70.1 %reduce-scatter.5.cloned.1.call-start = ((), (), s32[]{:S(2)}) async-start(), calls=%async_computation.3 | async-start | bytes 589824 | tf_op jit(solution)/shard_map/reduce_scatter | solution.py:44
  102.4 7.6 %copy-start.1 = (bf16[64,1,32,128]{0,2,3,1:T(8,128)(2,1)S(1)}, bf16[64,1,32,128]{0,2,3,1:T(8,128)(2,1)}, u32[]{:S(2)}) copy-start(bf16[64,1,32,128]{0,2,3,1:T(8,128)(2,1)} %copy.52) | copy-start | bytes 1572868
  111.6 1.4 copy-start.4
  122.5 2.2 copy-start.3
  124.6 107.1 %reduce-scatter.3.cloned.1.call-start = ((), (), s32[]{:S(2)}) async-start(), calls=%async_computation.2 | async-start | bytes 1114112 | tf_op jit(solution)/shard_map/reduce_scatter | solution.py:39
Sparse Core Ops, SparseCore 0:
  86.3 53.9 all-reduce.2
Sparse Core Ops, SparseCore 1:
  124.7 31.6 reduce-scatter.4
  159.2 72.4 reduce-scatter.2
where the time goes:
time: 242 us; the launch traced here: 241 us
  waiting for transfers between devices  95 us (39%)
  blocking collectives  53.3 us (22%)
  local copies, waits for them, and re-layouts  38.8 us (16%)
  matrix products  23.1 us (10%)
  between operations  15.7 us (6%)
  starting transfers between devices  9.59 us (4%)
  other arithmetic  5.19 us (2%)
    reduce_scatter x1, waiting for transfers between devices, body(): lax.psum_scatter(partial_out, 'cin', scatter_dimension=2, tiled=True)  73.9 us
    all_gather x1, blocking collectives, body(): g_panel = lax.all_gather(out_grad, 'cin', axis=2, tiled=True)  38 us
    all_gather x1, blocking collectives, body(): x_panel = lax.all_gather(activations, 'cout', axis=2, tiled=True)  15.2 us
    conv_general_dilated x2, matrix products, convolve(): lax.conv_general_dilated(field[None], kernel, (1, 1, 1), padding, dimensi...  14.8 us
    reduce_scatter x1, waiting for transfers between devices, body(): lax.psum_scatter(dx_partial, 'cout', scatter_dimension=2, tiled=True)  14.2 us
    conv_general_dilated x6, local copies, waits for them, and re-layouts, convolve(): lax.conv_general_dilated(field[None], kernel, (1, 1, 1), padding, dimensi...  11.7 us
    unnamed x15, local copies, waits for them, and re-layouts  9.87 us
    dot_general x27, matrix products, body(): jnp.einsum('cdhw,odhw->co', window, g_inner, preferred_element_type=jnp.f...  8.3 us
  transfers between devices with their start and end apart: 7, of which 3 were waited for; matrix products, arithmetic and copies ran while one was open for 27% of the time, Pallas kernels for 0%

commit v1 on v0

v1 whole, which is shorter than its diff:
```python
import math

import jax
import jax.numpy as jnp
from jax import lax
from jax.experimental import pallas as pl
from jax.experimental.pallas import tpu as pltpu
from jax.sharding import PartitionSpec as P

F32 = jnp.float32
BF16 = jnp.bfloat16
VMEM_LIMIT = 40 * 1024 * 1024


def shifted(plane, step):
    if step == 0:
        return plane
    width = plane.shape[-1]
    moved = pltpu.roll(plane.astype(F32), (-step) % width, plane.ndim - 1)
    lane = lax.broadcasted_iota(jnp.int32, plane.shape, plane.ndim - 1)
    edge = width - 1 if step > 0 else 0
    return jnp.where(lane == edge, 0.0, moved).astype(plane.dtype)


def stack_taps(planes, stacked):
    rows, channels, width = planes[0].shape
    for a, plane in enumerate(planes):
        value = plane[...]
        for c in range(3):
            moved = shifted(value, c - 1)
            at = (a * 3 + c) * channels
            for h in range(rows):
                stacked[at : at + channels, h * width : (h + 1) * width] = moved[h]


def add_row_taps(product, out, channels, rows, width):
    for h in range(rows):
        total = None
        for b in range(3):
            row = h + b - 1
            if 0 <= row < rows:
                part = product[b * channels : (b + 1) * channels, row * width : (row + 1) * width]
                total = part if total is None else total + part
        out[h] = total


def forward_kernel(low, mid, high, weights, out, stacked, product):
    rows, cin, width = mid.shape
    cout = weights.shape[-1]
    stack_taps((low, mid, high), stacked)
    blocks = [
        jnp.concatenate([weights[a, b, c] for a in range(3) for c in range(3)], axis=0)
        for b in range(3)
    ]
    kernel = jnp.concatenate([jnp.transpose(block.astype(F32)) for block in blocks], axis=0)
    product[...] = jnp.dot(kernel.astype(BF16), stacked[...], preferred_element_type=F32)
    add_row_taps(product, out, cout, rows, width)


def backward_kernel(low, mid, high, weights, out, stacked, product):
    rows, cout, width = mid.shape
    cin = weights.shape[-2]
    stack_taps((low, mid, high), stacked)
    kernel = jnp.concatenate(
        [
            jnp.concatenate(
                [weights[2 - a, 2 - b, 2 - c] for a in range(3) for c in range(3)], axis=1
            )
            for b in range(3)
        ],
        axis=0,
    )
    product[...] = jnp.dot(kernel, stacked[...], preferred_element_type=F32)
    add_row_taps(product, out, cin, rows, width)


def kernel_grad_kernel(low, mid, high, grad, out, stacked, shifted_grad):
    rows, cin, width = mid.shape
    cout = grad.shape[1]
    stack_taps((low, mid, high), stacked)
    for b in range(3):
        for h in range(rows):
            row = h - (b - 1)
            value = grad[row] if 0 <= row < rows else jnp.zeros((cout, width), BF16)
            shifted_grad[b * cout : (b + 1) * cout, h * width : (h + 1) * width] = value
    taps = lax.dot_general(
        stacked[...], shifted_grad[...], (((1,), (1,)), ((), ())), preferred_element_type=F32
    )
    half = taps.shape[0] // 2
    first = taps[:, : 2 * cout]
    second = jnp.concatenate([taps[:half, 2 * cout :], taps[half:, 2 * cout :]], axis=1)
    rest = out.shape[0] - first.shape[0] - half
    out[: 2 * half] = first
    out[2 * half : 3 * half] = second
    out[3 * half :] = jnp.zeros((rest, 2 * cout), F32)


def kernel_grad_finish(parts, out, scale):
    total = (parts[0] + parts[1]) + (parts[2] + parts[3])
    taps = (total * scale).astype(BF16)
    cin, cout = out.shape[-2:]
    half = 9 * cin // 2
    for a in range(3):
        for c in range(3):
            at = (a * 3 + c) * cin
            for b in range(2):
                out[a, b, c] = taps[at : at + cin, b * cout : (b + 1) * cout]
            for lo in range(at, at + cin, cin // 2):
                side = lo // half
                row = 2 * half + lo - side * half
                out[a, 2, c, lo - at : lo - at + cin // 2] = taps[
                    row : row + cin // 2, side * cout : (side + 1) * cout
                ]


def call(kernel, out, scratch, flops, *args):
    moved = sum(math.prod(a.shape) * a.dtype.itemsize for a in args)
    return pl.pallas_call(
        kernel,
        out_shape=out,
        scratch_shapes=scratch,
        compiler_params=pltpu.CompilerParams(vmem_limit_bytes=VMEM_LIMIT),
        cost_estimate=pl.CostEstimate(flops=flops, bytes_accessed=moved, transcendentals=0),
    )(*args)


def halos(plane, axis):
    count = lax.axis_size(axis)
    forward = [(i, i + 1) for i in range(count - 1)]
    backward = [(i + 1, i) for i in range(count - 1)]
    return lax.ppermute(plane, axis, forward), lax.ppermute(plane, axis, backward)


def body(activations, weights, out_grad):
    cin, cout = weights.shape[3:]
    width = activations.shape[-1]
    x_own = jnp.transpose(activations[:, 0], (1, 0, 2))
    g_own = jnp.transpose(out_grad[:, 0], (1, 0, 2))
    x_mid = lax.all_gather(x_own, "cout", axis=0, tiled=True)
    rows = x_mid.shape[0]
    voxels = rows * width
    flops = 2 * 27 * cin * cout * voxels
    x_low, x_high = halos(x_mid, "sp")

    partial_out = call(
        forward_kernel,
        jax.ShapeDtypeStruct((rows, cout, width), F32),
        [pltpu.VMEM((9 * cin, voxels), BF16), pltpu.VMEM((3 * cout, voxels), F32)],
        flops,
        x_low,
        x_mid,
        x_high,
        weights,
    )
    out_parts = lax.all_to_all(partial_out, "cin", 0, 0, tiled=True)

    g_mid = lax.all_gather(g_own, "cin", axis=0, tiled=True)
    g_low, g_high = halos(g_mid, "sp")
    packed_rows = -(-27 * cin // 2 // 32) * 32
    local_grad = call(
        kernel_grad_kernel,
        jax.ShapeDtypeStruct((packed_rows, 2 * cout), F32),
        [pltpu.VMEM((9 * cin, voxels), BF16), pltpu.VMEM((3 * cout, voxels), BF16)],
        flops,
        x_low,
        x_mid,
        x_high,
        g_mid,
    )
    depth = lax.axis_size("sp")
    grad_parts = lax.all_to_all(
        jnp.broadcast_to(local_grad, (depth,) + local_grad.shape), "sp", 0, 0, tiled=True
    )
    partial_dx = call(
        backward_kernel,
        jax.ShapeDtypeStruct((rows, cin, width), F32),
        [pltpu.VMEM((9 * cout, voxels), BF16), pltpu.VMEM((3 * cin, voxels), F32)],
        flops,
        g_low,
        g_mid,
        g_high,
        weights,
    )
    dx_parts = lax.all_to_all(partial_dx, "cout", 0, 0, tiled=True)

    scale = 1.0 / math.sqrt(depth * voxels)
    weight_grad = call(
        lambda parts, out: kernel_grad_finish(parts, out, scale),
        jax.ShapeDtypeStruct(weights.shape, BF16),
        [],
        27 * cin * cout * depth,
        grad_parts,
    )

    def total(parts, like, axis):
        summed = jnp.sum(parts.reshape((lax.axis_size(axis), -1) + parts.shape[1:]), axis=0)
        return jnp.transpose(summed, (1, 0, 2)).astype(BF16).reshape(like.shape)

    in_grad = total(dx_parts, activations, "cout")
    output = total(out_parts, out_grad, "cin")
    return output, in_grad, weight_grad


def solution(mesh):
    placed = (
        P("cin", "sp", "cout", None),
        P(None, None, None, "cin", "cout"),
        P("cout", "sp", "cin", None),
    )
    return jax.shard_map(
        body,
        mesh=mesh,
        in_specs=placed,
        out_specs=(
            P("cout", "sp", "cin", None),
            P("cin", "sp", "cout", None),
            P(None, None, None, "cin", "cout"),
        ),
        check_vma=False,
    )
```

time: 242 us -> 157 us (0.65)
  local copies, waits for them, and re-layouts: 38.8 us -> 3.08 us
  waiting for transfers between devices: 95 us -> 64.3 us
  matrix products: 23.1 us -> 0 us
  starting transfers between devices: 9.59 us -> 28 us
  between operations: 15.7 us -> 0.7 us
  Pallas kernels: 0 us -> 6.77 us
  other arithmetic: 5.19 us -> 0.1 us
    reduce_scatter x2 -> x0, waiting for transfers between devices: 88.1 us -> none  [the longest x1 73.9 us: body(): lax.psum_scatter(partial_out, 'cin', scatter_dimension=2, tiled=True)]
    all_to_all x0 -> x3, waiting for transfers between devices: none -> 54.3 us  [the longest x1 48.3 us: body(): out_parts = lax.all_to_all(partial_out, 'cin', 0, 0, tiled=True)]
    all_to_all x0 -> x3, starting transfers between devices: none -> 16.2 us  [the longest x1 7.31 us: body(): out_parts = lax.all_to_all(partial_out, 'cin', 0, 0, tiled=True)]
    conv_general_dilated x2 -> x0, matrix products: 14.8 us -> none  [convolve(): lax.conv_general_dilated(field[None], kernel, (1, 1, 1), padding, dimensi...]
    conv_general_dilated x6 -> x0, local copies, waits for them, and re-layouts: 11.7 us -> none  [convolve(): lax.conv_general_dilated(field[None], kernel, (1, 1, 1), padding, dimensi...]
    ppermute x4, waiting for transfers between devices: 0.01 us -> 9.97 us  [the longest x2 9.96 us: halos(): lax.ppermute(plane, axis, backward)]
    dot_general x27 -> x0, matrix products: 8.3 us -> none  [body(): jnp.einsum('cdhw,odhw->co', window, g_inner, preferred_element_type=jnp.f...]
    unnamed x15 -> x8, local copies, waits for them, and re-layouts: 9.87 us -> 2.06 us
  transfers between devices with their start and end apart: 7 -> 7, of which waited for: 3 -> 3; matrix products, arithmetic and copies ran while one was open for 27% -> 0% of each run, Pallas kernels for 0% -> 4%
where the time goes in v1:
time: 157 us; the launch traced here: 154 us
  waiting for transfers between devices  64.3 us (41%)
  blocking collectives  51.5 us (33%)
  starting transfers between devices  28 us (18%)
  Pallas kernels  6.77 us (4%)
  local copies, waits for them, and re-layouts  3.08 us (2%)
    all_to_all x1, waiting for transfers between devices, body(): out_parts = lax.all_to_all(partial_out, 'cin', 0, 0, tiled=True)  48.3 us
    all_gather x1, blocking collectives, body(): g_mid = lax.all_gather(g_own, 'cin', axis=0, tiled=True)  36.1 us
    all_gather x1, blocking collectives, body(): x_mid = lax.all_gather(x_own, 'cout', axis=0, tiled=True)  15.4 us
    ppermute x2, waiting for transfers between devices, halos(): lax.ppermute(plane, axis, backward)  9.96 us
    ppermute x2, starting transfers between devices, halos(): lax.ppermute(plane, axis, forward)  9.15 us
    all_to_all x1, starting transfers between devices, body(): out_parts = lax.all_to_all(partial_out, 'cin', 0, 0, tiled=True)  7.31 us
    pallas_call x4, Pallas kernels, call(): pl.pallas_call(kernel, out_shape=out, scratch_shapes=scratch, compiler_pa...  6.77 us
    all_to_all x1, waiting for transfers between devices, body(): dx_parts = lax.all_to_all(partial_dx, 'cout', 0, 0, tiled=True)  6.03 us
  transfers between devices with their start and end apart: 7, of which 3 were waited for; matrix products, arithmetic and copies ran while one was open for 0% of the time, Pallas kernels for 4%

profile of v1, /device:TPU:24, one launch (start us, length us, event | category | flops | bytes accessed | tf_op | source)
XLA Modules:
  0.0 154.4 jit_solution(6581784703914591920)
XLA Ops:
  0.6 0.8 copy.15
  1.4 0.0 copy-start.1
  1.4 15.4 %all_gather.6.mid = bf16[32,32,128]{2,1,0:T(8,128)(2,1)S(1)} all-gather(bf16[4,32,128]{2,1,0:T(8,128)(2,1)S(1)} %bitcast.26), channel_id=1, replica_groups=mesh['cin'=16,'cout'=8,'sp'=4] {'cout'}, dimensions={0}, use_global_device_ids=true | all-gather | bytes 294912 | tf_op jit(solution)/shard_map/all_gather | solution.py:139
  16.8 1.3 collective-permute-start.1
  18.1 4.6 %collective-permute-start = (bf16[32,32,128]{2,1,0:T(8,128)(2,1)S(1)}, bf16[32,32,128]{2,1,0:T(8,128)(2,1)S(1)}, u32[]{:S(2)}, u32[]{:S(2)}) collective-permute-start(bf16[32,32,128]{2,1,0:T(8,128)(2,1)S(1)} %all_gather.6.mid), channel_id=1, source_target_pairs={{0,1},{1,2},{2,3},{4,5},{5,6},{6,7},{8,9},{9,10},{10,11},{12,13},{... | collective-permute-start | bytes 786440 | tf_op jit(solution)/shard_map/ppermute | solution.py:131
  22.6 0.0 copy-done.1
  22.6 36.1 %all_gather.7.mid.grad = bf16[32,64,128]{2,1,0:T(8,128)(2,1)S(1)} all-gather(bf16[2,64,128]{2,1,0:T(8,128)(2,1)S(1)} %bitcast.27), channel_id=1, replica_groups=mesh['cin'=16,'cout'=8,'sp'=4] {'cin'}, dimensions={0}, use_global_device_ids=true | all-gather | bytes 557056 | tf_op jit(solution)/shard_map/all_gather | solution.py:157
  58.8 0.0 collective-permute-done.1.high
  58.8 0.0 collective-permute-done.low
  58.8 1.1 shard_map.60
  59.9 1.0 broadcast_in_dim.3
  60.9 0.0 copy-start
  60.9 4.4 %all-to-all-start.2 = ((f32[4,448,128]{2,1,0:T(8,128)}), f32[4,448,128]{2,1,0:T(8,128)S(1)}, u32[]{:S(2)}, u32[]{:S(2)}) async-start(f32[4,448,128]{2,1,0:T(8,128)} %broadcast_in_dim.3), calls=%async_computation.2 | async-start | bytes 1835008 | tf_op jit(solution)/shard_map/all_to_all | solution.py:171
  65.3 1.3 collective-permute-start.3
  66.6 4.6 %collective-permute-start.2 = (bf16[32,64,128]{2,1,0:T(8,128)(2,1)S(1)}, bf16[32,64,128]{2,1,0:T(8,128)(2,1)S(1)}, u32[]{:S(2)}, u32[]{:S(2)}) collective-permute-start(bf16[32,64,128]{2,1,0:T(8,128)(2,1)S(1)} %all_gather.7.mid.grad), channel_id=1, source_target_pairs={{0,1},{1,2},{2,3},{4,5},{5,6},{6,7},{8,9},{9,10},{10,11},{12,13},{... | collective-permute-start | bytes 1572872 | tf_op jit(solution)/shard_map/ppermute | solution.py:131
  71.2 10.0 %collective-permute-done.3.high = bf16[32,64,128]{2,1,0:T(8,128)(2,1)S(1)} collective-permute-done((bf16[32,64,128]{2,1,0:T(8,128)(2,1)S(1)}, bf16[32,64,128]{2,1,0:T(8,128)(2,1)S(1)}, u32[]{:S(2)}, u32[]{:S(2)}) %collective-permute-start.3) | collective-permute-done | bytes 524320 | tf_op jit(solution)/shard_map/ppermute | solution.py:131
  81.2 0.0 collective-permute-done.2.low
  81.2 0.0 copy-done
  81.2 2.6 %shard_map.59 = f32[32,32,128]{2,1,0:T(8,128)} custom-call(bf16[32,64,128]{2,1,0:T(8,128)(2,1)S(1)} %collective-permute-done.2.low, bf16[32,64,128]{2,1,0:T(8,128)(2,1)S(1)} %all_gather.7.mid.grad, bf16[32,64,128]{2,1,0:T(8,128)(2,1)S(1)} %collective-permute-done.3.high, bf16[3,3,3,32,64]{4,3,2,1,0:T(8,128)(2,1)S(1)} %copy-done), custom_call_target="tpu_custom_call" | custom-call | flops 452984832 | bytes 1683456 | tf_op jit(solution)/shard_map/pallas_call | solution.py:118
  83.8 0.0 all-to-all-done.2.parts
  83.8 4.5 %all-to-all-start.1 = ((f32[32,32,128]{2,1,0:T(8,128)}), f32[32,32,128]{2,1,0:T(8,128)S(1)}, u32[]{:S(2)}, u32[]{:S(2)}) async-start(f32[32,32,128]{2,1,0:T(8,128)} %shard_map.59), calls=%async_computation.1 | async-start | bytes 1048576 | tf_op jit(solution)/shard_map/all_to_all | solution.py:184
  88.3 2.2 %shard_map.58 = f32[32,64,128]{2,1,0:T(8,128)} custom-call(bf16[32,32,128]{2,1,0:T(8,128)(2,1)S(1)} %collective-permute-done.low, bf16[32,32,128]{2,1,0:T(8,128)(2,1)S(1)} %all_gather.6.mid, bf16[32,32,128]{2,1,0:T(8,128)(2,1)S(1)} %collective-permute-done.1.high, bf16[3,3,3,32,64]{4,3,2,1,0:T(8,128)(2,1)S(1)} %copy-done), custom_call_target="tpu_custom_call" | custom-call | flops 452984832 | bytes 897024 | tf_op jit(solution)/shard_map/pallas_call | solution.py:118
  90.6 6.0 %all-to-all-done.1 = f32[32,32,128]{2,1,0:T(8,128)S(1)} async-done(((f32[32,32,128]{2,1,0:T(8,128)}), f32[32,32,128]{2,1,0:T(8,128)S(1)}, u32[]{:S(2)}, u32[]{:S(2)}) %all-to-all-start.1) | async-done | bytes 524320 | tf_op jit(solution)/shard_map/all_to_all | solution.py:184
  96.6 7.3 %all-to-all-start = ((f32[32,64,128]{2,1,0:T(8,128)}), f32[32,64,128]{2,1,0:T(8,128)S(1)}, u32[]{:S(2)}, u32[]{:S(2)}) async-start(f32[32,64,128]{2,1,0:T(8,128)} %shard_map.58), calls=%async_computation | async-start | bytes 2097152 | tf_op jit(solution)/shard_map/all_to_all | solution.py:155
  103.9 0.8 shard_map.61
  104.8 0.6 copy.11
  105.4 48.3 %all-to-all-done = f32[32,64,128]{2,1,0:T(8,128)S(1)} async-done(((f32[32,64,128]{2,1,0:T(8,128)}), f32[32,64,128]{2,1,0:T(8,128)S(1)}, u32[]{:S(2)}, u32[]{:S(2)}) %all-to-all-start) | async-done | bytes 1048608 | tf_op jit(solution)/shard_map/all_to_all | solution.py:155
  153.7 0.1 reduce_sum.18
  153.7 0.6 copy.10
  (2 shorter events, 0.0 us)
Async XLA Ops:
  1.4 21.2 %copy-start.1 = (bf16[64,1,2,128]{3,2,1,0:T(2,128)(2,1)S(1)}, bf16[64,1,2,128]{3,2,1,0:T(2,128)(2,1)}, u32[]{:S(2)}) copy-start(bf16[64,1,2,128]{3,2,1,0:T(2,128)(2,1)} %param.5) | copy-start | bytes 98308
  16.8 42.0 %collective-permute-start.1 = (bf16[32,32,128]{2,1,0:T(8,128)(2,1)S(1)}, bf16[32,32,128]{2,1,0:T(8,128)(2,1)S(1)}, u32[]{:S(2)}, u32[]{:S(2)}) collective-permute-start(bf16[32,32,128]{2,1,0:T(8,128)(2,1)S(1)} %all_gather.6.mid), channel_id=1, source_target_pairs={{1,0},{2,1},{3,2},{5,4},{6,5},{7,6},{9,8},{10,9},{11,10},{13,12},{... | collective-permute-start | bytes 786440 | tf_op jit(solution)/shard_map/ppermute | solution.py:131
  18.1 40.7 %collective-permute-start = (bf16[32,32,128]{2,1,0:T(8,128)(2,1)S(1)}, bf16[32,32,128]{2,1,0:T(8,128)(2,1)S(1)}, u32[]{:S(2)}, u32[]{:S(2)}) collective-permute-start(bf16[32,32,128]{2,1,0:T(8,128)(2,1)S(1)} %all_gather.6.mid), channel_id=1, source_target_pairs={{0,1},{1,2},{2,3},{4,5},{5,6},{6,7},{8,9},{9,10},{10,11},{12,13},{... | collective-permute-start | bytes 786440 | tf_op jit(solution)/shard_map/ppermute | solution.py:131
  60.9 20.3 %copy-start = (bf16[3,3,3,32,64]{4,3,2,1,0:T(8,128)(2,1)S(1)}, bf16[3,3,3,32,64]{4,3,2,1,0:T(8,128)(2,1)}, u32[]{:S(2)}) copy-start(bf16[3,3,3,32,64]{4,3,2,1,0:T(8,128)(2,1)} %weights.3) | copy-start | bytes 331780
  60.9 22.9 %all-to-all-start.2 = ((f32[4,448,128]{2,1,0:T(8,128)}), f32[4,448,128]{2,1,0:T(8,128)S(1)}, u32[]{:S(2)}, u32[]{:S(2)}) async-start(f32[4,448,128]{2,1,0:T(8,128)} %broadcast_in_dim.3), calls=%async_computation.2 | async-start | bytes 1835008 | tf_op jit(solution)/shard_map/all_to_all | solution.py:171
  65.3 15.8 %collective-permute-start.3 = (bf16[32,64,128]{2,1,0:T(8,128)(2,1)S(1)}, bf16[32,64,128]{2,1,0:T(8,128)(2,1)S(1)}, u32[]{:S(2)}, u32[]{:S(2)}) collective-permute-start(bf16[32,64,128]{2,1,0:T(8,128)(2,1)S(1)} %all_gather.7.mid.grad), channel_id=1, source_target_pairs={{1,0},{2,1},{3,2},{5,4},{6,5},{7,6},{9,8},{10,9},{11,10},{13,12},{... | collective-permute-start | bytes 1572872 | tf_op jit(solution)/shard_map/ppermute | solution.py:131
  66.6 14.6 %collective-permute-start.2 = (bf16[32,64,128]{2,1,0:T(8,128)(2,1)S(1)}, bf16[32,64,128]{2,1,0:T(8,128)(2,1)S(1)}, u32[]{:S(2)}, u32[]{:S(2)}) collective-permute-start(bf16[32,64,128]{2,1,0:T(8,128)(2,1)S(1)} %all_gather.7.mid.grad), channel_id=1, source_target_pairs={{0,1},{1,2},{2,3},{4,5},{5,6},{6,7},{8,9},{9,10},{10,11},{12,13},{... | collective-permute-start | bytes 1572872 | tf_op jit(solution)/shard_map/ppermute | solution.py:131
  83.8 12.8 %all-to-all-start.1 = ((f32[32,32,128]{2,1,0:T(8,128)}), f32[32,32,128]{2,1,0:T(8,128)S(1)}, u32[]{:S(2)}, u32[]{:S(2)}) async-start(f32[32,32,128]{2,1,0:T(8,128)} %shard_map.59), calls=%async_computation.1 | async-start | bytes 1048576 | tf_op jit(solution)/shard_map/all_to_all | solution.py:184
  96.6 57.1 %all-to-all-start = ((f32[32,64,128]{2,1,0:T(8,128)}), f32[32,64,128]{2,1,0:T(8,128)S(1)}, u32[]{:S(2)}, u32[]{:S(2)}) async-start(f32[32,64,128]{2,1,0:T(8,128)} %shard_map.58), calls=%async_computation | async-start | bytes 2097152 | tf_op jit(solution)/shard_map/all_to_all | solution.py:155

commit v2 on v1

--- a/solution.py
+++ b/solution.py
@@ -1,3 +1,4 @@
+import functools
 import math
 
 import jax
@@ -44,7 +45,7 @@
         out[h] = total
 
 
-def forward_kernel(low, mid, high, weights, out, stacked, product):
+def forward_kernel(place, low, mid, high, weights, own, ahead, behind, far_a, far_b, stacked, product):
     rows, cin, width = mid.shape
     cout = weights.shape[-1]
     stack_taps((low, mid, high), stacked)
@@ -53,8 +54,40 @@
         for b in range(3)
     ]
     kernel = jnp.concatenate([jnp.transpose(block.astype(F32)) for block in blocks], axis=0)
-    product[...] = jnp.dot(kernel.astype(BF16), stacked[...], preferred_element_type=F32)
-    add_row_taps(product, out, cout, rows, width)
+    product[:, width:-width] = jnp.dot(
+        kernel.astype(BF16), stacked[...], preferred_element_type=F32
+    )
+    edge = jnp.zeros((product.shape[0], width), F32)
+    product[:, :width] = edge
+    product[:, -width:] = edge
+    repeats, each = own.shape[:2]
+    ways = rows // (repeats * each)
+    for slot in range(ways):
+        kind = lax.rem(place[0] + slot, ways)
+        for q in range(repeats):
+            for e in range(each):
+                row = (q * ways + kind) * each + e
+                total = None
+                for b in range(3):
+                    at = pl.multiple_of((row + b) * width, width)
+                    part = product[b * cout : (b + 1) * cout, pl.ds(at, width)]
+                    total = part if total is None else total + part
+                if slot == 0:
+                    own[q, e] = total
+                elif slot == 1:
+                    ahead[q, e] = total
+                elif slot == 2:
+                    far_a[q, e] = total[: cout // 2]
+                    far_b[q, e] = total[cout // 2 :]
+                else:
+                    behind[q, e] = total
+
+
+def near_sum_kernel(own, ahead, behind, far_a, far_b, out):
+    half = far_a.shape[2]
+    near = own[...] + (ahead[...] + behind[...])
+    out[:, :, :half] = near[:, :, :half] + far_a[...]
+    out[:, :, half:] = near[:, :, half:] + far_b[...]
 
 
 def backward_kernel(low, mid, high, weights, out, stacked, product):
@@ -95,9 +128,8 @@
     out[3 * half :] = jnp.zeros((rest, 2 * cout), F32)
 
 
-def kernel_grad_finish(parts, out, scale):
-    total = (parts[0] + parts[1]) + (parts[2] + parts[3])
-    taps = (total * scale).astype(BF16)
+def kernel_grad_finish(scale, near, far, out):
+    taps = ((near[...] + far[...]) * scale).astype(BF16)
     cin, cout = out.shape[-2:]
     half = 9 * cin // 2
     for a in range(3):
@@ -115,9 +147,11 @@
 
 def call(kernel, out, scratch, flops, *args):
     moved = sum(math.prod(a.shape) * a.dtype.itemsize for a in args)
+    specs = [pl.BlockSpec(memory_space=pltpu.SMEM if a.ndim == 1 else pltpu.VMEM) for a in args]
     return pl.pallas_call(
         kernel,
         out_shape=out,
+        in_specs=specs,
         scratch_shapes=scratch,
         compiler_params=pltpu.CompilerParams(vmem_limit_bytes=VMEM_LIMIT),
         cost_estimate=pl.CostEstimate(flops=flops, bytes_accessed=moved, transcendentals=0),
@@ -131,30 +165,69 @@
     return lax.ppermute(plane, axis, forward), lax.ppermute(plane, axis, backward)
 
 
+def around(block, axis, step):
+    count = lax.axis_size(axis)
+    return lax.ppermute(block, axis, [(i, (i + step) % count) for i in range(count)])
+
+
+def exchange(blocks, axis, groups=None):
+    return lax.all_to_all(blocks, axis, 0, 0, tiled=True, axis_index_groups=groups)
+
+
+def gather(block, axis, count, groups=None):
+    copies = jnp.broadcast_to(block[None], (count,) + block.shape)
+    return exchange(copies, axis, groups).reshape((-1,) + block.shape[1:])
+
+
 def body(activations, weights, out_grad):
     cin, cout = weights.shape[3:]
     width = activations.shape[-1]
+    ring = lax.axis_size("cin")
+    depth = lax.axis_size("sp")
+    ways = 4
+    repeats = ring // ways
+    apart = [[ways * q + r for q in range(repeats)] for r in range(ways)]
     x_own = jnp.transpose(activations[:, 0], (1, 0, 2))
     g_own = jnp.transpose(out_grad[:, 0], (1, 0, 2))
+    each = g_own.shape[0]
+
+    g_mid = gather(g_own, "cin", ring)
     x_mid = lax.all_gather(x_own, "cout", axis=0, tiled=True)
     rows = x_mid.shape[0]
     voxels = rows * width
     flops = 2 * 27 * cin * cout * voxels
     x_low, x_high = halos(x_mid, "sp")
 
-    partial_out = call(
+    piece = jax.ShapeDtypeStruct((repeats, each, cout, width), F32)
+    half_piece = jax.ShapeDtypeStruct((repeats, each, cout // 2, width), F32)
+    place = lax.axis_index("cin").astype(jnp.int32).reshape(1)
+    own, ahead, behind, far_a, far_b = call(
         forward_kernel,
-        jax.ShapeDtypeStruct((rows, cout, width), F32),
-        [pltpu.VMEM((9 * cin, voxels), BF16), pltpu.VMEM((3 * cout, voxels), F32)],
+        (piece, piece, piece, half_piece, half_piece),
+        [
+            pltpu.VMEM((9 * cin, voxels), BF16),
+            pltpu.VMEM((3 * cout, voxels + 2 * width), F32),
+        ],
         flops,
+        place,
         x_low,
         x_mid,
         x_high,
         weights,
     )
-    out_parts = lax.all_to_all(partial_out, "cin", 0, 0, tiled=True)
-
-    g_mid = lax.all_gather(g_own, "cin", axis=0, tiled=True)
+    near_sum = call(
+        near_sum_kernel,
+        piece,
+        [],
+        4 * math.prod(piece.shape),
+        own,
+        around(ahead, "cin", 1),
+        around(behind, "cin", -1),
+        around(far_a, "cin", 2),
+        around(far_b, "cin", -2),
+    )
+    out_parts = exchange(near_sum, "cin", apart)
+
     g_low, g_high = halos(g_mid, "sp")
     packed_rows = -(-27 * cin // 2 // 32) * 32
     local_grad = call(
@@ -167,10 +240,8 @@
         x_high,
         g_mid,
     )
-    depth = lax.axis_size("sp")
-    grad_parts = lax.all_to_all(
-        jnp.broadcast_to(local_grad, (depth,) + local_grad.shape), "sp", 0, 0, tiled=True
-    )
+    pair_grad = local_grad + lax.ppermute(local_grad, "sp", [(i, i ^ 1) for i in range(depth)])
+    far_grad = lax.ppermute(pair_grad, "sp", [(i, depth - 1 - i) for i in range(depth)])
     partial_dx = call(
         backward_kernel,
         jax.ShapeDtypeStruct((rows, cin, width), F32),
@@ -181,24 +252,24 @@
         g_high,
         weights,
     )
-    dx_parts = lax.all_to_all(partial_dx, "cout", 0, 0, tiled=True)
+    dx_parts = exchange(partial_dx, "cout")
 
     scale = 1.0 / math.sqrt(depth * voxels)
     weight_grad = call(
-        lambda parts, out: kernel_grad_finish(parts, out, scale),
+        functools.partial(kernel_grad_finish, scale),
         jax.ShapeDtypeStruct(weights.shape, BF16),
         [],
-        27 * cin * cout * depth,
-        grad_parts,
-    )
-
-    def total(parts, like, axis):
-        summed = jnp.sum(parts.reshape((lax.axis_size(axis), -1) + parts.shape[1:]), axis=0)
+        27 * cin * cout * 2,
+        pair_grad,
+        far_grad,
+    )
+
+    def total(parts, like):
+        parts = parts.reshape((-1, like.shape[2]) + parts.shape[-2:])
+        summed = jnp.sum(parts, axis=0)
         return jnp.transpose(summed, (1, 0, 2)).astype(BF16).reshape(like.shape)
 
-    in_grad = total(dx_parts, activations, "cout")
-    output = total(out_parts, out_grad, "cin")
-    return output, in_grad, weight_grad
+    return total(out_parts, out_grad), total(dx_parts, activations), weight_grad
 
 
 def solution(mesh):

time: 157 us -> 117 us (0.75)
  blocking collectives: 51.5 us -> 13 us
  waiting for transfers between devices: 64.3 us -> 31.7 us
  starting transfers between devices: 28 us -> 59.7 us
    all_to_all x3, waiting for transfers between devices: 54.3 us -> 0.01 us  [exchange(): lax.all_to_all(blocks, axis, 0, 0, tiled=True, axis_index_groups=groups)]
    all_gather x1 -> x0, blocking collectives: 36.1 us -> none  [body(): g_mid = lax.all_gather(g_own, 'cin', axis=0, tiled=True)]
    ppermute x0 -> x6, starting transfers between devices: none -> 21.5 us  [the longest x4 15 us: around(): lax.ppermute(block, axis, [(i, (i + step) % count) for i in range(count)])]
    ppermute x0 -> x6, waiting for transfers between devices: none -> 14.9 us  [the longest x1 8.16 us: body(): lax.ppermute(pair_grad, 'sp', [(i, depth - 1 - i) for i in range(depth)])]
    all_to_all x3, starting transfers between devices: 16.2 us -> 28.8 us  [exchange(): lax.all_to_all(blocks, axis, 0, 0, tiled=True, axis_index_groups=groups)]
    ppermute x2, waiting for transfers between devices: 0.01 us -> 8.51 us  [halos(): lax.ppermute(plane, axis, forward)]
    all_gather x1, blocking collectives: 15.4 us -> 13 us  [body(): x_mid = lax.all_gather(x_own, 'cout', axis=0, tiled=True)]
    ppermute x2, starting transfers between devices: 9.15 us -> 6.8 us  [halos(): lax.ppermute(plane, axis, forward)]
  transfers between devices with their start and end apart: 7 -> 13, of which waited for: 3 -> 7; matrix products, arithmetic and copies ran while one was open for 0% -> 1% of each run, Pallas kernels for 4% -> 6%
where the time goes in v2:
time: 117 us; the launch traced here: 115 us
  starting transfers between devices  59.7 us (51%)
  waiting for transfers between devices  31.7 us (27%)
  blocking collectives  13 us (11%)
  Pallas kernels  6.95 us (6%)
  local copies, waits for them, and re-layouts  2.98 us (3%)
    all_to_all x3, starting transfers between devices, exchange(): lax.all_to_all(blocks, axis, 0, 0, tiled=True, axis_index_groups=groups)  28.8 us
    ppermute x4, starting transfers between devices, around(): lax.ppermute(block, axis, [(i, (i + step) % count) for i in range(count)])  15 us
    all_gather x1, blocking collectives, body(): x_mid = lax.all_gather(x_own, 'cout', axis=0, tiled=True)  13 us
    ppermute x2, waiting for transfers between devices, halos(): lax.ppermute(plane, axis, forward)  8.51 us
    ppermute x2, waiting for transfers between devices, halos(): lax.ppermute(plane, axis, backward)  8.27 us
    ppermute x1, waiting for transfers between devices, body(): lax.ppermute(pair_grad, 'sp', [(i, depth - 1 - i) for i in range(depth)])  8.16 us
    pallas_call x5, Pallas kernels, call(): pl.pallas_call(kernel, out_shape=out, in_specs=specs, scratch_shapes=scra...  6.95 us
    ppermute x2, starting transfers between devices, halos(): lax.ppermute(plane, axis, forward)  6.8 us
  transfers between devices with their start and end apart: 13, of which 7 were waited for; matrix products, arithmetic and copies ran while one was open for 1% of the time, Pallas kernels for 6%

profile of v2, /device:TPU:24, one launch (start us, length us, event | category | flops | bytes accessed | tf_op | source)
XLA Modules:
  0.0 115.2 jit_solution(9167269491892532474)
XLA Ops:
  0.6 0.8 copy.9
  1.4 0.9 broadcast_in_dim.2
  2.3 0.0 copy-start.1
  2.3 15.3 %all-to-all-start.1 = ((bf16[16,2,64,128]{3,2,1,0:T(8,128)(2,1)}), bf16[16,2,64,128]{3,2,1,0:T(8,128)(2,1)S(1)}, u32[]{:S(2)}, u32[]{:S(2)}) async-start(bf16[16,2,64,128]{3,2,1,0:T(8,128)(2,1)} %broadcast_in_dim.2), calls=%async_computation.1 | async-start | bytes 1048576 | tf_op jit(solution)/shard_map/all_to_all | solution.py:174
  17.6 0.0 copy-done.1
  17.7 0.0 copy-start
  17.7 13.0 %all_gather.3.mid = bf16[32,32,128]{2,1,0:T(8,128)(2,1)S(1)} all-gather(bf16[4,32,128]{2,1,0:T(8,128)(2,1)S(1)} %bitcast.28), channel_id=1, replica_groups=mesh['cin'=16,'cout'=8,'sp'=4] {'cout'}, dimensions={0}, use_global_device_ids=true | all-gather | bytes 294912 | tf_op jit(solution)/shard_map/all_gather | solution.py:195
  30.7 3.4 %collective-permute-start = (bf16[32,32,128]{2,1,0:T(8,128)(2,1)S(1)}, bf16[32,32,128]{2,1,0:T(8,128)(2,1)S(1)}, u32[]{:S(2)}, u32[]{:S(2)}) collective-permute-start(bf16[32,32,128]{2,1,0:T(8,128)(2,1)S(1)} %all_gather.3.mid), channel_id=1, source_target_pairs={{0,1},{1,2},{2,3},{4,5},{5,6},{6,7},{8,9},{9,10},{10,11},{12,13},{... | collective-permute-start | bytes 786440 | tf_op jit(solution)/shard_map/ppermute | solution.py:165
  34.1 1.3 %collective-permute-start.1 = (bf16[32,32,128]{2,1,0:T(8,128)(2,1)S(1)}, bf16[32,32,128]{2,1,0:T(8,128)(2,1)S(1)}, u32[]{:S(2)}, u32[]{:S(2)}) collective-permute-start(bf16[32,32,128]{2,1,0:T(8,128)(2,1)S(1)} %all_gather.3.mid), channel_id=1, source_target_pairs={{1,0},{2,1},{3,2},{5,4},{6,5},{7,6},{9,8},{10,9},{11,10},{13,12},{... | collective-permute-start | bytes 786440 | tf_op jit(solution)/shard_map/ppermute | solution.py:165
  35.4 4.7 %collective-permute-done.low = bf16[32,32,128]{2,1,0:T(8,128)(2,1)S(1)} collective-permute-done((bf16[32,32,128]{2,1,0:T(8,128)(2,1)S(1)}, bf16[32,32,128]{2,1,0:T(8,128)(2,1)S(1)}, u32[]{:S(2)}, u32[]{:S(2)}) %collective-permute-start) | collective-permute-done | bytes 262176 | tf_op jit(solution)/shard_map/ppermute | solution.py:165
  40.1 4.1 %collective-permute-done.1.high = bf16[32,32,128]{2,1,0:T(8,128)(2,1)S(1)} collective-permute-done((bf16[32,32,128]{2,1,0:T(8,128)(2,1)S(1)}, bf16[32,32,128]{2,1,0:T(8,128)(2,1)S(1)}, u32[]{:S(2)}, u32[]{:S(2)}) %collective-permute-start.1) | collective-permute-done | bytes 262176 | tf_op jit(solution)/shard_map/ppermute | solution.py:165
  44.2 0.0 copy-done
  44.2 1.7 %shard_map.58 = (f32[4,2,64,128]{3,2,1,0:T(8,128)S(1)}, f32[4,2,64,128]{3,2,1,0:T(8,128)S(1)}, f32[4,2,64,128]{3,2,1,0:T(8,128)S(1)}, f32[4,2,32,128]{3,2,1,0:T(8,128)S(1)}, f32[4,2,32,128]{3,2,1,0:T(8,128)S(1)}) custom-call(s32[1]{0:T(128)} %bitcast.place, bf16[32,32,128]{2,1,0:T(8,128)(2,1)S(1)} %collective-permute-done.low, ...), custom_call_target="tpu_custom_call" | custom-call | flops 452984832 | bytes 897028 | tf_op jit(solution)/shard_map/pallas_call | solution.py:151
  45.9 3.8 %collective-permute-start.2 = (f32[4,2,64,128]{3,2,1,0:T(8,128)S(1)}, f32[4,2,64,128]{3,2,1,0:T(8,128)S(1)}, u32[]{:S(2)}, u32[]{:S(2)}) collective-permute-start(f32[4,2,64,128]{3,2,1,0:T(8,128)S(1)} %get-tuple-element.9), channel_id=1, source_target_pairs={{0,32},{32,64},{64,96},{96,128},{128,160},{160,192},{192,224},{224... | collective-permute-start | bytes 786440 | tf_op jit(solution)/shard_map/ppermute | solution.py:170
  49.7 3.2 %collective-permute-start.3 = (f32[4,2,64,128]{3,2,1,0:T(8,128)S(1)}, f32[4,2,64,128]{3,2,1,0:T(8,128)S(1)}, u32[]{:S(2)}, u32[]{:S(2)}) collective-permute-start(f32[4,2,64,128]{3,2,1,0:T(8,128)S(1)} %get-tuple-element.10), channel_id=1, source_target_pairs={{0,480},{32,0},{64,32},{96,64},{128,96},{160,128},{192,160},{224,1... | collective-permute-start | bytes 786440 | tf_op jit(solution)/shard_map/ppermute | solution.py:170
  53.0 3.5 %collective-permute-start.4 = (f32[4,2,32,128]{3,2,1,0:T(8,128)S(1)}, f32[4,2,32,128]{3,2,1,0:T(8,128)S(1)}, u32[]{:S(2)}, u32[]{:S(2)}) collective-permute-start(f32[4,2,32,128]{3,2,1,0:T(8,128)S(1)} %get-tuple-element.11), channel_id=1, source_target_pairs={{0,64},{32,96},{64,128},{96,160},{128,192},{160,224},{192,256},{22... | collective-permute-start | bytes 393224 | tf_op jit(solution)/shard_map/ppermute | solution.py:170
  56.5 4.4 %collective-permute-start.5 = (f32[4,2,32,128]{3,2,1,0:T(8,128)S(1)}, f32[4,2,32,128]{3,2,1,0:T(8,128)S(1)}, u32[]{:S(2)}, u32[]{:S(2)}) collective-permute-start(f32[4,2,32,128]{3,2,1,0:T(8,128)S(1)} %get-tuple-element.12), channel_id=1, source_target_pairs={{0,448},{32,480},{64,0},{96,32},{128,64},{160,96},{192,128},{224,1... | collective-permute-start | bytes 393224 | tf_op jit(solution)/shard_map/ppermute | solution.py:170
  60.9 3.1 %collective-permute-done.4.far_a = f32[4,2,32,128]{3,2,1,0:T(8,128)S(1)} collective-permute-done((f32[4,2,32,128]{3,2,1,0:T(8,128)S(1)}, f32[4,2,32,128]{3,2,1,0:T(8,128)S(1)}, u32[]{:S(2)}, u32[]{:S(2)}) %collective-permute-start.4) | collective-permute-done | bytes 131104 | tf_op jit(solution)/shard_map/ppermute | solution.py:170
  64.0 3.7 %collective-permute-done.5.far_b = f32[4,2,32,128]{3,2,1,0:T(8,128)S(1)} collective-permute-done((f32[4,2,32,128]{3,2,1,0:T(8,128)S(1)}, f32[4,2,32,128]{3,2,1,0:T(8,128)S(1)}, u32[]{:S(2)}, u32[]{:S(2)}) %collective-permute-start.5) | collective-permute-done | bytes 131104 | tf_op jit(solution)/shard_map/ppermute | solution.py:170
  67.7 0.0 collective-permute-done.2.ahead
  67.7 0.0 collective-permute-done.3.behind
  67.7 0.8 shard_map.59
  68.5 0.0 all-to-all-done.1
  68.5 9.0 %all-to-all-start = ((f32[4,2,64,128]{3,2,1,0:T(8,128)}), f32[4,2,64,128]{3,2,1,0:T(8,128)S(1)}, u32[]{:S(2)}, u32[]{:S(2)}) async-start(f32[4,2,64,128]{3,2,1,0:T(8,128)} %shard_map.59), calls=%async_computation | async-start | bytes 524288 | tf_op jit(solution)/shard_map/all_to_all | solution.py:174
  77.5 3.4 %collective-permute-start.6 = (bf16[32,64,128]{2,1,0:T(8,128)(2,1)S(1)}, bf16[32,64,128]{2,1,0:T(8,128)(2,1)S(1)}, u32[]{:S(2)}, u32[]{:S(2)}) collective-permute-start(bf16[32,64,128]{2,1,0:T(8,128)(2,1)S(1)} %bitcast.21), channel_id=1, source_target_pairs={{0,1},{1,2},{2,3},{4,5},{5,6},{6,7},{8,9},{9,10},{10,11},{12,13},{... | collective-permute-start | bytes 1572872 | tf_op jit(solution)/shard_map/ppermute | solution.py:165
  80.9 1.3 %collective-permute-start.7 = (bf16[32,64,128]{2,1,0:T(8,128)(2,1)S(1)}, bf16[32,64,128]{2,1,0:T(8,128)(2,1)S(1)}, u32[]{:S(2)}, u32[]{:S(2)}) collective-permute-start(bf16[32,64,128]{2,1,0:T(8,128)(2,1)S(1)} %bitcast.22), channel_id=1, source_target_pairs={{1,0},{2,1},{3,2},{5,4},{6,5},{7,6},{9,8},{10,9},{11,10},{13,12},{... | collective-permute-start | bytes 1572872 | tf_op jit(solution)/shard_map/ppermute | solution.py:165
  82.2 1.1 shard_map.61
  83.3 4.6 %collective-permute-start.8 = (f32[448,128]{1,0:T(8,128)S(1)}, f32[448,128]{1,0:T(8,128)S(1)}, u32[]{:S(2)}, u32[]{:S(2)}) collective-permute-start(f32[448,128]{1,0:T(8,128)S(1)} %shard_map.61), channel_id=1, source_target_pairs={{0,1},{1,0},{2,3},{3,2},{4,5},{5,4},{6,7},{7,6},{8,9},{9,8},{10,11... | collective-permute-start | bytes 688136 | tf_op jit(solution)/shard_map/ppermute | solution.py:243
  87.8 3.8 %collective-permute-done.6.low = bf16[32,64,128]{2,1,0:T(8,128)(2,1)S(1)} collective-permute-done((bf16[32,64,128]{2,1,0:T(8,128)(2,1)S(1)}, bf16[32,64,128]{2,1,0:T(8,128)(2,1)S(1)}, u32[]{:S(2)}, u32[]{:S(2)}) %collective-permute-start.6) | collective-permute-done | bytes 524320 | tf_op jit(solution)/shard_map/ppermute | solution.py:165
  91.6 4.1 %collective-permute-done.7.high = bf16[32,64,128]{2,1,0:T(8,128)(2,1)S(1)} collective-permute-done((bf16[32,64,128]{2,1,0:T(8,128)(2,1)S(1)}, bf16[32,64,128]{2,1,0:T(8,128)(2,1)S(1)}, u32[]{:S(2)}, u32[]{:S(2)}) %collective-permute-start.7) | collective-permute-done | bytes 524320 | tf_op jit(solution)/shard_map/ppermute | solution.py:165
  95.8 2.6 %shard_map.60 = f32[32,32,128]{2,1,0:T(8,128)} custom-call(bf16[32,64,128]{2,1,0:T(8,128)(2,1)S(1)} %collective-permute-done.6.low, bf16[32,64,128]{2,1,0:T(8,128)(2,1)S(1)} %bitcast.24, bf16[32,64,128]{2,1,0:T(8,128)(2,1)S(1)} %collective-permute-done.7.high, bf16[3,3,3,32,64]{4,3,2,1,0:T(8,128)(2,1)S(1)} %copy-done), custom_call_target="tpu_custom_call" | custom-call | flops 452984832 | bytes 1683456 | tf_op jit(solution)/shard_map/pallas_call | solution.py:151
  98.4 0.0 all-to-all-done
  98.4 4.5 %all-to-all-start.2 = ((f32[32,32,128]{2,1,0:T(8,128)}), f32[32,32,128]{2,1,0:T(8,128)S(1)}, u32[]{:S(2)}, u32[]{:S(2)}) async-start(f32[32,32,128]{2,1,0:T(8,128)} %shard_map.60), calls=%async_computation.2 | async-start | bytes 1048576 | tf_op jit(solution)/shard_map/all_to_all | solution.py:174
  102.9 0.0 collective-permute-done.8
  102.9 1.9 %collective-permute-start.9 = (f32[448,128]{1,0:T(8,128)S(1)}, f32[448,128]{1,0:T(8,128)S(1)}, u32[]{:S(2)}, u32[]{:S(2)}) collective-permute-start(f32[448,128]{1,0:T(8,128)S(1)} %add.3.near), channel_id=1, source_target_pairs={{0,3},{1,2},{2,1},{3,0},{4,7},{5,6},{6,5},{7,4},{8,11},{9,10},{10,... | collective-permute-start | bytes 688136 | tf_op jit(solution)/shard_map/ppermute | solution.py:244
  104.9 0.6 copy.10
  105.5 8.2 %collective-permute-done.9.far = f32[448,128]{1,0:T(8,128)S(1)} collective-permute-done((f32[448,128]{1,0:T(8,128)S(1)}, f32[448,128]{1,0:T(8,128)S(1)}, u32[]{:S(2)}, u32[]{:S(2)}) %collective-permute-start.9) | collective-permute-done | bytes 229408 | tf_op jit(solution)/shard_map/ppermute | solution.py:244
  113.7 0.8 shard_map.62
  114.5 0.0 all-to-all-done.2
  114.5 0.6 copy.11
  (4 shorter events, 0.1 us)
Async XLA Ops:
  2.3 15.3 %copy-start.1 = (bf16[32,1,4,128]{3,2,1,0:T(4,128)(2,1)S(1)}, bf16[32,1,4,128]{3,2,1,0:T(4,128)(2,1)}, u32[]{:S(2)}) copy-start(bf16[32,1,4,128]{3,2,1,0:T(4,128)(2,1)} %param.3) | copy-start | bytes 98308
  2.3 66.2 %all-to-all-start.1 = ((bf16[16,2,64,128]{3,2,1,0:T(8,128)(2,1)}), bf16[16,2,64,128]{3,2,1,0:T(8,128)(2,1)S(1)}, u32[]{:S(2)}, u32[]{:S(2)}) async-start(bf16[16,2,64,128]{3,2,1,0:T(8,128)(2,1)} %broadcast_in_dim.2), calls=%async_computation.1 | async-start | bytes 1048576 | tf_op jit(solution)/shard_map/all_to_all | solution.py:174
  17.7 26.6 %copy-start = (bf16[3,3,3,32,64]{4,3,2,1,0:T(8,128)(2,1)S(1)}, bf16[3,3,3,32,64]{4,3,2,1,0:T(8,128)(2,1)}, u32[]{:S(2)}) copy-start(bf16[3,3,3,32,64]{4,3,2,1,0:T(8,128)(2,1)} %weights.3) | copy-start | bytes 331780
  30.7 9.4 %collective-permute-start = (bf16[32,32,128]{2,1,0:T(8,128)(2,1)S(1)}, bf16[32,32,128]{2,1,0:T(8,128)(2,1)S(1)}, u32[]{:S(2)}, u32[]{:S(2)}) collective-permute-start(bf16[32,32,128]{2,1,0:T(8,128)(2,1)S(1)} %all_gather.3.mid), channel_id=1, source_target_pairs={{0,1},{1,2},{2,3},{4,5},{5,6},{6,7},{8,9},{9,10},{10,11},{12,13},{... | collective-permute-start | bytes 786440 | tf_op jit(solution)/shard_map/ppermute | solution.py:165
  34.1 10.2 %collective-permute-start.1 = (bf16[32,32,128]{2,1,0:T(8,128)(2,1)S(1)}, bf16[32,32,128]{2,1,0:T(8,128)(2,1)S(1)}, u32[]{:S(2)}, u32[]{:S(2)}) collective-permute-start(bf16[32,32,128]{2,1,0:T(8,128)(2,1)S(1)} %all_gather.3.mid), channel_id=1, source_target_pairs={{1,0},{2,1},{3,2},{5,4},{6,5},{7,6},{9,8},{10,9},{11,10},{13,12},{... | collective-permute-start | bytes 786440 | tf_op jit(solution)/shard_map/ppermute | solution.py:165
  45.9 21.8 %collective-permute-start.2 = (f32[4,2,64,128]{3,2,1,0:T(8,128)S(1)}, f32[4,2,64,128]{3,2,1,0:T(8,128)S(1)}, u32[]{:S(2)}, u32[]{:S(2)}) collective-permute-start(f32[4,2,64,128]{3,2,1,0:T(8,128)S(1)} %get-tuple-element.9), channel_id=1, source_target_pairs={{0,32},{32,64},{64,96},{96,128},{128,160},{160,192},{192,224},{224... | collective-permute-start | bytes 786440 | tf_op jit(solution)/shard_map/ppermute | solution.py:170
  49.7 18.0 %collective-permute-start.3 = (f32[4,2,64,128]{3,2,1,0:T(8,128)S(1)}, f32[4,2,64,128]{3,2,1,0:T(8,128)S(1)}, u32[]{:S(2)}, u32[]{:S(2)}) collective-permute-start(f32[4,2,64,128]{3,2,1,0:T(8,128)S(1)} %get-tuple-element.10), channel_id=1, source_target_pairs={{0,480},{32,0},{64,32},{96,64},{128,96},{160,128},{192,160},{224,1... | collective-permute-start | bytes 786440 | tf_op jit(solution)/shard_map/ppermute | solution.py:170
  53.0 11.1 %collective-permute-start.4 = (f32[4,2,32,128]{3,2,1,0:T(8,128)S(1)}, f32[4,2,32,128]{3,2,1,0:T(8,128)S(1)}, u32[]{:S(2)}, u32[]{:S(2)}) collective-permute-start(f32[4,2,32,128]{3,2,1,0:T(8,128)S(1)} %get-tuple-element.11), channel_id=1, source_target_pairs={{0,64},{32,96},{64,128},{96,160},{128,192},{160,224},{192,256},{22... | collective-permute-start | bytes 393224 | tf_op jit(solution)/shard_map/ppermute | solution.py:170
  56.5 11.2 %collective-permute-start.5 = (f32[4,2,32,128]{3,2,1,0:T(8,128)S(1)}, f32[4,2,32,128]{3,2,1,0:T(8,128)S(1)}, u32[]{:S(2)}, u32[]{:S(2)}) collective-permute-start(f32[4,2,32,128]{3,2,1,0:T(8,128)S(1)} %get-tuple-element.12), channel_id=1, source_target_pairs={{0,448},{32,480},{64,0},{96,32},{128,64},{160,96},{192,128},{224,1... | collective-permute-start | bytes 393224 | tf_op jit(solution)/shard_map/ppermute | solution.py:170
  68.5 29.9 %all-to-all-start = ((f32[4,2,64,128]{3,2,1,0:T(8,128)}), f32[4,2,64,128]{3,2,1,0:T(8,128)S(1)}, u32[]{:S(2)}, u32[]{:S(2)}) async-start(f32[4,2,64,128]{3,2,1,0:T(8,128)} %shard_map.59), calls=%async_computation | async-start | bytes 524288 | tf_op jit(solution)/shard_map/all_to_all | solution.py:174
  77.5 14.1 %collective-permute-start.6 = (bf16[32,64,128]{2,1,0:T(8,128)(2,1)S(1)}, bf16[32,64,128]{2,1,0:T(8,128)(2,1)S(1)}, u32[]{:S(2)}, u32[]{:S(2)}) collective-permute-start(bf16[32,64,128]{2,1,0:T(8,128)(2,1)S(1)} %bitcast.21), channel_id=1, source_target_pairs={{0,1},{1,2},{2,3},{4,5},{5,6},{6,7},{8,9},{9,10},{10,11},{12,13},{... | collective-permute-start | bytes 1572872 | tf_op jit(solution)/shard_map/ppermute | solution.py:165
  80.9 14.9 %collective-permute-start.7 = (bf16[32,64,128]{2,1,0:T(8,128)(2,1)S(1)}, bf16[32,64,128]{2,1,0:T(8,128)(2,1)S(1)}, u32[]{:S(2)}, u32[]{:S(2)}) collective-permute-start(bf16[32,64,128]{2,1,0:T(8,128)(2,1)S(1)} %bitcast.22), channel_id=1, source_target_pairs={{1,0},{2,1},{3,2},{5,4},{6,5},{7,6},{9,8},{10,9},{11,10},{13,12},{... | collective-permute-start | bytes 1572872 | tf_op jit(solution)/shard_map/ppermute | solution.py:165
  83.3 19.6 %collective-permute-start.8 = (f32[448,128]{1,0:T(8,128)S(1)}, f32[448,128]{1,0:T(8,128)S(1)}, u32[]{:S(2)}, u32[]{:S(2)}) collective-permute-start(f32[448,128]{1,0:T(8,128)S(1)} %shard_map.61), channel_id=1, source_target_pairs={{0,1},{1,0},{2,3},{3,2},{4,5},{5,4},{6,7},{7,6},{8,9},{9,8},{10,11... | collective-permute-start | bytes 688136 | tf_op jit(solution)/shard_map/ppermute | solution.py:243
  98.4 16.1 %all-to-all-start.2 = ((f32[32,32,128]{2,1,0:T(8,128)}), f32[32,32,128]{2,1,0:T(8,128)S(1)}, u32[]{:S(2)}, u32[]{:S(2)}) async-start(f32[32,32,128]{2,1,0:T(8,128)} %shard_map.60), calls=%async_computation.2 | async-start | bytes 1048576 | tf_op jit(solution)/shard_map/all_to_all | solution.py:174
  102.9 10.8 %collective-permute-start.9 = (f32[448,128]{1,0:T(8,128)S(1)}, f32[448,128]{1,0:T(8,128)S(1)}, u32[]{:S(2)}, u32[]{:S(2)}) collective-permute-start(f32[448,128]{1,0:T(8,128)S(1)} %add.3.near), channel_id=1, source_target_pairs={{0,3},{1,2},{2,1},{3,0},{4,7},{5,6},{6,5},{7,4},{8,11},{9,10},{10,... | collective-permute-start | bytes 688136 | tf_op jit(solution)/shard_map/ppermute | solution.py:244

commit v3 on v2

--- a/solution.py
+++ b/solution.py
@@ -26,7 +26,7 @@
 def stack_taps(planes, stacked):
     rows, channels, width = planes[0].shape
     for a, plane in enumerate(planes):
-        value = plane[...]
+        value = plane
         for c in range(3):
             moved = shifted(value, c - 1)
             at = (a * 3 + c) * channels
@@ -34,21 +34,20 @@
                 stacked[at : at + channels, h * width : (h + 1) * width] = moved[h]
 
 
-def add_row_taps(product, out, channels, rows, width):
-    for h in range(rows):
-        total = None
-        for b in range(3):
-            row = h + b - 1
-            if 0 <= row < rows:
-                part = product[b * channels : (b + 1) * channels, row * width : (row + 1) * width]
-                total = part if total is None else total + part
-        out[h] = total
-
-
-def forward_kernel(place, low, mid, high, weights, own, ahead, behind, far_a, far_b, stacked, product):
-    rows, cin, width = mid.shape
+def row_total(product, channels, row, width):
+    total = None
+    for b in range(3):
+        at = pl.multiple_of((row + b) * width, width)
+        part = product[b * channels : (b + 1) * channels, pl.ds(at, width)]
+        total = part if total is None else total + part
+    return total
+
+
+def forward_kernel(place, planes, weights, own, ahead, far, behind, stacked, product):
+    cin, width = planes.shape[-2:]
+    rows = planes.shape[0] * planes.shape[2]
     cout = weights.shape[-1]
-    stack_taps((low, mid, high), stacked)
+    stack_taps([planes[:, a].reshape(rows, cin, width) for a in range(3)], stacked)
     blocks = [
         jnp.concatenate([weights[a, b, c] for a in range(3) for c in range(3)], axis=0)
         for b in range(3)
@@ -67,33 +66,21 @@
         for q in range(repeats):
             for e in range(each):
                 row = (q * ways + kind) * each + e
-                total = None
-                for b in range(3):
-                    at = pl.multiple_of((row + b) * width, width)
-                    part = product[b * cout : (b + 1) * cout, pl.ds(at, width)]
-                    total = part if total is None else total + part
-                if slot == 0:
-                    own[q, e] = total
-                elif slot == 1:
-                    ahead[q, e] = total
-                elif slot == 2:
-                    far_a[q, e] = total[: cout // 2]
-                    far_b[q, e] = total[cout // 2 :]
-                else:
-                    behind[q, e] = total
-
-
-def near_sum_kernel(own, ahead, behind, far_a, far_b, out):
-    half = far_a.shape[2]
-    near = own[...] + (ahead[...] + behind[...])
-    out[:, :, :half] = near[:, :, :half] + far_a[...]
-    out[:, :, half:] = near[:, :, half:] + far_b[...]
-
-
-def backward_kernel(low, mid, high, weights, out, stacked, product):
+                (own, ahead, far, behind)[slot][q, e] = row_total(product, cout, row, width)
+
+
+def sum_kernel(own, far, ahead, behind, out):
+    out[...] = (own[...] + far[...]) + (ahead[...] + behind[...])
+
+
+def pair_sum_kernel(kept, came, out):
+    out[...] = kept[...] + came[...]
+
+
+def backward_kernel(place, low, mid, high, weights, kept, handed, stacked, product):
     rows, cout, width = mid.shape
     cin = weights.shape[-2]
-    stack_taps((low, mid, high), stacked)
+    stack_taps((low[...], mid[...], high[...]), stacked)
     kernel = jnp.concatenate(
         [
             jnp.concatenate(
@@ -103,14 +90,23 @@
         ],
         axis=0,
     )
-    product[...] = jnp.dot(kernel, stacked[...], preferred_element_type=F32)
-    add_row_taps(product, out, cin, rows, width)
-
-
-def kernel_grad_kernel(low, mid, high, grad, out, stacked, shifted_grad):
-    rows, cin, width = mid.shape
+    product[:, width:-width] = jnp.dot(kernel, stacked[...], preferred_element_type=F32)
+    edge = jnp.zeros((product.shape[0], width), F32)
+    product[:, :width] = edge
+    product[:, -width:] = edge
+    chips, share = kept.shape[:2]
+    core = lax.rem(place[0], 2)
+    for part, at_core in ((kept, core), (handed, 1 - core)):
+        for chip in range(chips):
+            for e in range(share):
+                part[chip, e] = row_total(product, cin, (chip * 2 + at_core) * share + e, width)
+
+
+def kernel_grad_kernel(planes, grad, out, stacked, shifted_grad):
+    rows = grad.shape[0]
+    cin, width = planes.shape[-2:]
     cout = grad.shape[1]
-    stack_taps((low, mid, high), stacked)
+    stack_taps([planes[:, a].reshape(rows, cin, width) for a in range(3)], stacked)
     for b in range(3):
         for h in range(rows):
             row = h - (b - 1)
@@ -170,13 +166,18 @@
     return lax.ppermute(block, axis, [(i, (i + step) % count) for i in range(count)])
 
 
+def around_by_core(block):
+    ring, cores = lax.axis_size("cin"), lax.axis_size("cout")
+    pairs = [
+        (z * cores + y, (z + (2 if y % 2 == 0 else -2)) % ring * cores + y)
+        for z in range(ring)
+        for y in range(cores)
+    ]
+    return lax.ppermute(block, ("cin", "cout"), pairs)
+
+
 def exchange(blocks, axis, groups=None):
     return lax.all_to_all(blocks, axis, 0, 0, tiled=True, axis_index_groups=groups)
-
-
-def gather(block, axis, count, groups=None):
-    copies = jnp.broadcast_to(block[None], (count,) + block.shape)
-    return exchange(copies, axis, groups).reshape((-1,) + block.shape[1:])
 
 
 def body(activations, weights, out_grad):
@@ -191,43 +192,30 @@
     g_own = jnp.transpose(out_grad[:, 0], (1, 0, 2))
     each = g_own.shape[0]
 
-    g_mid = gather(g_own, "cin", ring)
-    x_mid = lax.all_gather(x_own, "cout", axis=0, tiled=True)
-    rows = x_mid.shape[0]
+    x_low, x_high = halos(x_own, "sp")
+    g_copies = jnp.broadcast_to(g_own[None], (ring,) + g_own.shape)
+    g_copies, x_low, x_high = lax.optimization_barrier((g_copies, x_low, x_high))
+    g_mid = exchange(g_copies, "cin").reshape((-1,) + g_own.shape[1:])
+    x_all = lax.all_gather(jnp.stack([x_low, x_own, x_high]), "cout", axis=0)
+    rows = x_all.shape[0] * x_all.shape[2]
     voxels = rows * width
     flops = 2 * 27 * cin * cout * voxels
-    x_low, x_high = halos(x_mid, "sp")
 
     piece = jax.ShapeDtypeStruct((repeats, each, cout, width), F32)
-    half_piece = jax.ShapeDtypeStruct((repeats, each, cout // 2, width), F32)
     place = lax.axis_index("cin").astype(jnp.int32).reshape(1)
-    own, ahead, behind, far_a, far_b = call(
+    own, ahead, far, behind = call(
         forward_kernel,
-        (piece, piece, piece, half_piece, half_piece),
+        (piece, piece, piece, piece),
         [
             pltpu.VMEM((9 * cin, voxels), BF16),
             pltpu.VMEM((3 * cout, voxels + 2 * width), F32),
         ],
         flops,
         place,
-        x_low,
-        x_mid,
-        x_high,
+        x_all,
         weights,
     )
-    near_sum = call(
-        near_sum_kernel,
-        piece,
-        [],
-        4 * math.prod(piece.shape),
-        own,
-        around(ahead, "cin", 1),
-        around(behind, "cin", -1),
-        around(far_a, "cin", 2),
-        around(far_b, "cin", -2),
-    )
-    out_parts = exchange(near_sum, "cin", apart)
-
+    g_mid, own = lax.optimization_barrier((g_mid, own))
     g_low, g_high = halos(g_mid, "sp")
     packed_rows = -(-27 * cin // 2 // 32) * 32
     local_grad = call(
@@ -235,24 +223,54 @@
         jax.ShapeDtypeStruct((packed_rows, 2 * cout), F32),
         [pltpu.VMEM((9 * cin, voxels), BF16), pltpu.VMEM((3 * cout, voxels), BF16)],
         flops,
-        x_low,
-        x_mid,
-        x_high,
+        x_all,
         g_mid,
     )
-    pair_grad = local_grad + lax.ppermute(local_grad, "sp", [(i, i ^ 1) for i in range(depth)])
-    far_grad = lax.ppermute(pair_grad, "sp", [(i, depth - 1 - i) for i in range(depth)])
-    partial_dx = call(
+    local_grad, own = lax.optimization_barrier((local_grad, own))
+    near_sum = call(
+        sum_kernel,
+        piece,
+        [],
+        4 * math.prod(piece.shape),
+        own,
+        around_by_core(far),
+        around(ahead, "cin", 1),
+        around(behind, "cin", -1),
+    )
+    near_grad = lax.ppermute(local_grad, "sp", [(i, i ^ 1) for i in range(depth)])
+    near_sum, g_mid = lax.optimization_barrier((near_sum, g_mid))
+    near_grad, g_mid = lax.optimization_barrier((near_grad, g_mid))
+    out_parts = exchange(near_sum, "cin", apart)
+
+    cores = 2
+    chips = lax.axis_size("cout") // cores
+    share = rows // (chips * cores)
+    place = lax.axis_index("cout").astype(jnp.int32).reshape(1)
+    chunks = jax.ShapeDtypeStruct((chips, share, cin, width), F32)
+    chunk = jax.ShapeDtypeStruct((share, cin, width), F32)
+    kept, handed = call(
         backward_kernel,
-        jax.ShapeDtypeStruct((rows, cin, width), F32),
-        [pltpu.VMEM((9 * cout, voxels), BF16), pltpu.VMEM((3 * cin, voxels), F32)],
+        (chunks, chunks),
+        [
+            pltpu.VMEM((9 * cout, voxels), BF16),
+            pltpu.VMEM((3 * cin, voxels + 2 * width), F32),
+        ],
         flops,
+        place,
         g_low,
         g_mid,
         g_high,
         weights,
     )
-    dx_parts = exchange(partial_dx, "cout")
+    came = lax.ppermute(handed, "cout", [(i, i ^ 1) for i in range(chips * cores)])
+    pair_dx = call(pair_sum_kernel, chunks, [], math.prod(chunks.shape), kept, came)
+    pair_grad = local_grad + near_grad
+    far_grad = lax.ppermute(pair_grad, "sp", [(i, depth - 1 - i) for i in range(depth)])
+    pair_dx, out_parts = lax.optimization_barrier((pair_dx, out_parts))
+    same_core = [[cores * y + core for y in range(chips)] for core in range(cores)]
+    dx_parts = exchange(
+        pair_dx.reshape((chips * share, cin, width)), "cout", same_core
+    ).reshape(chunks.shape)
 
     scale = 1.0 / math.sqrt(depth * voxels)
     weight_grad = call(
@@ -264,12 +282,11 @@
         far_grad,
     )
 
-    def total(parts, like):
-        parts = parts.reshape((-1, like.shape[2]) + parts.shape[-2:])
-        summed = jnp.sum(parts, axis=0)
+    def placed_as(summed, like):
         return jnp.transpose(summed, (1, 0, 2)).astype(BF16).reshape(like.shape)
 
-    return total(out_parts, out_grad), total(dx_parts, activations), weight_grad
+    out_total = jnp.sum(out_parts, axis=0)
+    return placed_as(out_total, out_grad), placed_as(jnp.sum(dx_parts, axis=0), activations), weight_grad
 
 
 def solution(mesh):

time: 117 us -> 105 us (0.90)
  the two profiles are of different devices: /device:TPU:24 before, /device:TPU:34 now
where the time goes in v3:
time: 105 us
  starting transfers between devices  58.5 us (56%)
  waiting for transfers between devices  19.5 us (19%)
  blocking collectives  14.1 us (13%)
  Pallas kernels  7.95 us (8%)
  local copies, waits for them, and re-layouts  3.67 us (3%)
    all_to_all x3, starting transfers between devices, exchange(): lax.all_to_all(blocks, axis, 0, 0, tiled=True, axis_index_groups=groups)  28.6 us
    all_gather x1, blocking collectives, body(): x_all = lax.all_gather(jnp.stack([x_low, x_own, x_high]), 'cout', axis=0)  14.1 us
    all_to_all x3, waiting for transfers between devices, exchange(): lax.all_to_all(blocks, axis, 0, 0, tiled=True, axis_index_groups=groups)  9.56 us
    pallas_call x6, Pallas kernels, call(): pl.pallas_call(kernel, out_shape=out, in_specs=specs, scratch_shapes=scra...  7.95 us
    ppermute x2, starting transfers between devices, halos(): lax.ppermute(plane, axis, forward)  6.8 us
    ppermute x1, waiting for transfers between devices, body(): lax.ppermute(local_grad, 'sp', [(i, i ^ 1) for i in range(depth)])  6.57 us
    ppermute x2, starting transfers between devices, around(): lax.ppermute(block, axis, [(i, (i + step) % count) for i in range(count)])  6.5 us
    ppermute x2, starting transfers between devices, halos(): lax.ppermute(plane, axis, backward)  4.87 us
  transfers between devices with their start and end apart: 13, of which 5 were waited for; matrix products, arithmetic and copies ran while one was open for 1% of the time, Pallas kernels for 8%

profile of v3, /device:TPU:34, one launch (start us, length us, event | category | flops | bytes accessed | tf_op | source)
XLA Modules:
  0.0 104.7 jit_solution(6180498974757748174)
XLA Ops:
  0.6 0.0 copy-start.4
  0.6 0.8 copy.14
  1.4 3.4 %collective-permute-start = (bf16[4,32,128]{2,1,0:T(8,128)(2,1)S(1)}, bf16[4,32,128]{2,1,0:T(8,128)(2,1)S(1)}, u32[]{:S(2)}, u32[]{:S(2)}) collective-permute-start(bf16[4,32,128]{2,1,0:T(8,128)(2,1)S(1)} %bitcast.38), channel_id=1, source_target_pairs={{0,1},{1,2},{2,3},{4,5},{5,6},{6,7},{8,9},{9,10},{10,11},{12,13},{... | collective-permute-start | bytes 98312 | tf_op jit(solution)/shard_map/ppermute | solution.py:161
  4.8 2.4 %collective-permute-start.1 = (bf16[4,32,128]{2,1,0:T(8,128)(2,1)S(1)}, bf16[4,32,128]{2,1,0:T(8,128)(2,1)S(1)}, u32[]{:S(2)}, u32[]{:S(2)}) collective-permute-start(bf16[4,32,128]{2,1,0:T(8,128)(2,1)S(1)} %bitcast.39), channel_id=1, source_target_pairs={{1,0},{2,1},{3,2},{5,4},{6,5},{7,6},{9,8},{10,9},{11,10},{13,12},{... | collective-permute-start | bytes 98312 | tf_op jit(solution)/shard_map/ppermute | solution.py:161
  7.3 0.0 copy-done.4
  7.3 0.0 collective-permute-done
  7.3 3.3 %collective-permute-done.1 = bf16[4,32,128]{2,1,0:T(8,128)(2,1)S(1)} collective-permute-done((bf16[4,32,128]{2,1,0:T(8,128)(2,1)S(1)}, bf16[4,32,128]{2,1,0:T(8,128)(2,1)S(1)}, u32[]{:S(2)}, u32[]{:S(2)}) %collective-permute-start.1) | collective-permute-done | bytes 32800 | tf_op jit(solution)/shard_map/ppermute | solution.py:161
  10.6 0.9 broadcast_in_dim.2
  11.5 15.2 %all-to-all-start = ((bf16[16,2,64,128]{3,2,1,0:T(8,128)(2,1)}), bf16[16,2,64,128]{3,2,1,0:T(8,128)(2,1)S(1)}, u32[]{:S(2)}, u32[]{:S(2)}) async-start(bf16[16,2,64,128]{3,2,1,0:T(8,128)(2,1)} %broadcast_in_dim.2), calls=%async_computation | async-start | bytes 1048576 | tf_op jit(solution)/shard_map/all_to_all | solution.py:180
  26.8 0.0 copy-start.2
  26.8 14.1 %all-gather = bf16[24,4,32,128]{3,2,1,0:T(8,128)(2,1)S(1)} all-gather(bf16[3,4,32,128]{3,2,1,0:T(8,128)(2,1)S(1)} %pad_maximum_fusion), channel_id=2, replica_groups=mesh['cin'=16,'cout'=8,'sp'=4] {'cout'}, dimensions={0}, use_global_device_ids=true | all-gather | bytes 884736 | tf_op jit(solution)/shard_map/all_gather | solution.py:199
  40.9 0.0 copy-done.2
  40.9 2.5 %shard_map.58 = (f32[4,2,64,128]{3,2,1,0:T(8,128)S(1)}, f32[4,2,64,128]{3,2,1,0:T(8,128)}, f32[4,2,64,128]{3,2,1,0:T(8,128)}, f32[4,2,64,128]{3,2,1,0:T(8,128)}) custom-call(s32[1]{0:T(128)} %bitcast.7.place, bf16[8,3,4,32,128]{4,3,2,1,0:T(8,128)(2,1)S(1)} %bitcast.33, bf16[3,3,3,32,64]{4,3,2,1,0:T(8,128)(2,1)S(1)} %copy-done.2), custom_call_target="tpu_custom_call" | custom-call | flops 452984832 | bytes 897028 | tf_op jit(solution)/shard_map/pallas_call | solution.py:147
  43.4 4.3 %collective-permute-start.4 = (f32[4,2,64,128]{3,2,1,0:T(8,128)}, f32[4,2,64,128]{3,2,1,0:T(8,128)S(1)}, u32[]{:S(2)}, u32[]{:S(2)}) collective-permute-start(f32[4,2,64,128]{3,2,1,0:T(8,128)} %get-tuple-element.30), channel_id=1, source_target_pairs={{0,64},{4,452},{8,72},{12,460},{16,80},{20,468},{24,88},{28,476},{... | collective-permute-start | bytes 786440 | tf_op jit(solution)/shard_map/ppermute | solution.py:176
  47.7 4.6 %collective-permute-start.5 = (f32[4,2,64,128]{3,2,1,0:T(8,128)}, f32[4,2,64,128]{3,2,1,0:T(8,128)S(1)}, u32[]{:S(2)}, u32[]{:S(2)}) collective-permute-start(f32[4,2,64,128]{3,2,1,0:T(8,128)} %get-tuple-element.31), channel_id=1, source_target_pairs={{0,32},{32,64},{64,96},{96,128},{128,160},{160,192},{192,224},{224... | collective-permute-start | bytes 786440 | tf_op jit(solution)/shard_map/ppermute | solution.py:166
  52.3 1.9 %collective-permute-start.6 = (f32[4,2,64,128]{3,2,1,0:T(8,128)}, f32[4,2,64,128]{3,2,1,0:T(8,128)S(1)}, u32[]{:S(2)}, u32[]{:S(2)}) collective-permute-start(f32[4,2,64,128]{3,2,1,0:T(8,128)} %get-tuple-element.32), channel_id=1, source_target_pairs={{0,480},{32,0},{64,32},{96,64},{128,96},{160,128},{192,160},{224,1... | collective-permute-start | bytes 786440 | tf_op jit(solution)/shard_map/ppermute | solution.py:166
  54.2 0.0 all-to-all-done
  54.2 2.4 %collective-permute-start.7 = (bf16[32,64,128]{2,1,0:T(8,128)(2,1)S(1)}, bf16[32,64,128]{2,1,0:T(8,128)(2,1)S(1)}, u32[]{:S(2)}, u32[]{:S(2)}) collective-permute-start(bf16[32,64,128]{2,1,0:T(8,128)(2,1)S(1)} %bitcast.29), channel_id=1, source_target_pairs={{1,0},{2,1},{3,2},{5,4},{6,5},{7,6},{9,8},{10,9},{11,10},{13,12},{... | collective-permute-start | bytes 1572872 | tf_op jit(solution)/shard_map/ppermute | solution.py:161
  56.7 3.4 %collective-permute-start.2 = (bf16[32,64,128]{2,1,0:T(8,128)(2,1)S(1)}, bf16[32,64,128]{2,1,0:T(8,128)(2,1)S(1)}, u32[]{:S(2)}, u32[]{:S(2)}) collective-permute-start(bf16[32,64,128]{2,1,0:T(8,128)(2,1)S(1)} %bitcast.30), channel_id=1, source_target_pairs={{0,1},{1,2},{2,3},{4,5},{5,6},{6,7},{8,9},{9,10},{10,11},{12,13},{... | collective-permute-start | bytes 1572872 | tf_op jit(solution)/shard_map/ppermute | solution.py:161
  60.1 1.1 %shard_map.59 = f32[448,128]{1,0:T(8,128)S(1)} custom-call(bf16[8,3,4,32,128]{4,3,2,1,0:T(8,128)(2,1)S(1)} %bitcast.34, bf16[32,64,128]{2,1,0:T(8,128)(2,1)S(1)} %bitcast.31), custom_call_target="tpu_custom_call" | custom-call | flops 452984832 | bytes 1310720 | tf_op jit(solution)/shard_map/pallas_call | solution.py:147
  61.2 0.0 copy-start
  61.2 0.7 copy-done
  61.9 0.0 collective-permute-done.4.far
  61.9 0.1 collective-permute-done.5.ahead
  61.9 0.0 collective-permute-done.6.behind
  61.9 0.7 shard_map.60
  62.7 0.0 copy-start.1
  62.7 0.0 copy-start.3
  62.7 9.5 %all-to-all-start.1 = ((f32[4,2,64,128]{3,2,1,0:T(8,128)}), f32[4,2,64,128]{3,2,1,0:T(8,128)S(1)}, u32[]{:S(2)}, u32[]{:S(2)}) async-start(f32[4,2,64,128]{3,2,1,0:T(8,128)} %shard_map.60), calls=%async_computation.1 | async-start | bytes 524288 | tf_op jit(solution)/shard_map/all_to_all | solution.py:180
  72.2 0.0 copy-done.1
  72.2 2.4 %collective-permute-start.3 = (f32[448,128]{1,0:T(8,128)S(1)}, f32[448,128]{1,0:T(8,128)S(1)}, u32[]{:S(2)}, u32[]{:S(2)}) collective-permute-start(f32[448,128]{1,0:T(8,128)S(1)} %copy-done.1), channel_id=1, source_target_pairs={{0,1},{1,0},{2,3},{3,2},{4,5},{5,4},{6,7},{7,6},{8,9},{9,8},{10,11... | collective-permute-start | bytes 688136 | tf_op jit(solution)/shard_map/ppermute | solution.py:240
  74.7 6.6 %collective-permute-done.3 = f32[448,128]{1,0:T(8,128)S(1)} collective-permute-done((f32[448,128]{1,0:T(8,128)S(1)}, f32[448,128]{1,0:T(8,128)S(1)}, u32[]{:S(2)}, u32[]{:S(2)}) %collective-permute-start.3) | collective-permute-done | bytes 229408 | tf_op jit(solution)/shard_map/ppermute | solution.py:240
  81.2 0.0 collective-permute-done.7.high
  81.2 0.0 collective-permute-done.2.low
  81.3 0.0 copy-done.3
  81.3 2.0 %shard_map.61 = (f32[4,4,32,128]{3,2,1,0:T(8,128)S(1)}, f32[4,4,32,128]{3,2,1,0:T(8,128)S(1)}) custom-call(s32[1]{0:T(128)} %bitcast.place, bf16[32,64,128]{2,1,0:T(8,128)(2,1)S(1)} %collective-permute-done.2.low, bf16[32,64,128]{2,1,0:T(8,128)(2,1)S(1)} %bitcast.32, bf16[32,64,128]{2,1,0:T(8,128)(2,1)S(1)} %collective-permute-done.7.high, ...), custom_call_target="tpu_custom_call" | custom-call | flops 452984832 | bytes 1683460 | tf_op jit(solution)/shard_map/pallas_call | solution.py:147
  83.3 1.9 %collective-permute-start.8 = (f32[4,4,32,128]{3,2,1,0:T(8,128)S(1)}, f32[4,4,32,128]{3,2,1,0:T(8,128)S(1)}, u32[]{:S(2)}, u32[]{:S(2)}) collective-permute-start(f32[4,4,32,128]{3,2,1,0:T(8,128)S(1)} %get-tuple-element.36), channel_id=1, source_target_pairs={{0,4},{4,0},{8,12},{12,8},{16,20},{20,16},{24,28},{28,24},{1,5},{5... | collective-permute-start | bytes 786440 | tf_op jit(solution)/shard_map/ppermute | solution.py:265
  85.3 3.1 %collective-permute-start.9 = (f32[448,128]{1,0:T(8,128)S(1)}, f32[448,128]{1,0:T(8,128)S(1)}, u32[]{:S(2)}, u32[]{:S(2)}) collective-permute-start(f32[448,128]{1,0:T(8,128)S(1)} %add.3.near), channel_id=1, source_target_pairs={{0,3},{1,2},{2,1},{3,0},{4,7},{5,6},{6,5},{7,4},{8,11},{9,10},{10,... | collective-permute-start | bytes 688136 | tf_op jit(solution)/shard_map/ppermute | solution.py:268
  88.4 0.0 collective-permute-done.8.came
  88.4 0.7 shard_map.62
  89.1 4.4 %all-to-all-done.1 = f32[4,2,64,128]{3,2,1,0:T(8,128)S(1)} async-done(((f32[4,2,64,128]{3,2,1,0:T(8,128)}), f32[4,2,64,128]{3,2,1,0:T(8,128)S(1)}, u32[]{:S(2)}, u32[]{:S(2)}) %all-to-all-start.1) | async-done | bytes 262176 | tf_op jit(solution)/shard_map/all_to_all | solution.py:180
  93.5 3.8 %all-to-all-start.2 = ((f32[16,32,128]{2,1,0:T(8,128)}), f32[16,32,128]{2,1,0:T(8,128)S(1)}, u32[]{:S(2)}, u32[]{:S(2)}) async-start(f32[16,32,128]{2,1,0:T(8,128)} %bitcast.14), calls=%async_computation.2 | async-start | bytes 524288 | tf_op jit(solution)/shard_map/all_to_all | solution.py:180
  97.3 0.0 collective-permute-done.9.far
  97.3 0.8 shard_map.63
  98.2 0.6 copy.10
  98.8 5.2 %all-to-all-done.2 = f32[16,32,128]{2,1,0:T(8,128)S(1)} async-done(((f32[16,32,128]{2,1,0:T(8,128)}), f32[16,32,128]{2,1,0:T(8,128)S(1)}, u32[]{:S(2)}, u32[]{:S(2)}) %all-to-all-start.2) | async-done | bytes 262176 | tf_op jit(solution)/shard_map/all_to_all | solution.py:180
  104.0 0.6 copy.11
  (5 shorter events, 0.1 us)
Async XLA Ops:
  0.6 6.6 %copy-start.4 = (bf16[64,1,2,128]{3,2,1,0:T(2,128)(2,1)S(1)}, bf16[64,1,2,128]{3,2,1,0:T(2,128)(2,1)}, u32[]{:S(2)}) copy-start(bf16[64,1,2,128]{3,2,1,0:T(2,128)(2,1)} %param.5) | copy-start | bytes 98308
  1.4 5.9 %collective-permute-start = (bf16[4,32,128]{2,1,0:T(8,128)(2,1)S(1)}, bf16[4,32,128]{2,1,0:T(8,128)(2,1)S(1)}, u32[]{:S(2)}, u32[]{:S(2)}) collective-permute-start(bf16[4,32,128]{2,1,0:T(8,128)(2,1)S(1)} %bitcast.38), channel_id=1, source_target_pairs={{0,1},{1,2},{2,3},{4,5},{5,6},{6,7},{8,9},{9,10},{10,11},{12,13},{... | collective-permute-start | bytes 98312 | tf_op jit(solution)/shard_map/ppermute | solution.py:161
  4.8 5.8 %collective-permute-start.1 = (bf16[4,32,128]{2,1,0:T(8,128)(2,1)S(1)}, bf16[4,32,128]{2,1,0:T(8,128)(2,1)S(1)}, u32[]{:S(2)}, u32[]{:S(2)}) collective-permute-start(bf16[4,32,128]{2,1,0:T(8,128)(2,1)S(1)} %bitcast.39), channel_id=1, source_target_pairs={{1,0},{2,1},{3,2},{5,4},{6,5},{7,6},{9,8},{10,9},{11,10},{13,12},{... | collective-permute-start | bytes 98312 | tf_op jit(solution)/shard_map/ppermute | solution.py:161
  11.5 42.7 %all-to-all-start = ((bf16[16,2,64,128]{3,2,1,0:T(8,128)(2,1)}), bf16[16,2,64,128]{3,2,1,0:T(8,128)(2,1)S(1)}, u32[]{:S(2)}, u32[]{:S(2)}) async-start(bf16[16,2,64,128]{3,2,1,0:T(8,128)(2,1)} %broadcast_in_dim.2), calls=%async_computation | async-start | bytes 1048576 | tf_op jit(solution)/shard_map/all_to_all | solution.py:180
  26.8 14.1 %copy-start.2 = (bf16[3,3,3,32,64]{4,3,2,1,0:T(8,128)(2,1)S(1)}, bf16[3,3,3,32,64]{4,3,2,1,0:T(8,128)(2,1)}, u32[]{:S(2)}) copy-start(bf16[3,3,3,32,64]{4,3,2,1,0:T(8,128)(2,1)} %weights.3) | copy-start | bytes 331780
  43.4 18.4 %collective-permute-start.4 = (f32[4,2,64,128]{3,2,1,0:T(8,128)}, f32[4,2,64,128]{3,2,1,0:T(8,128)S(1)}, u32[]{:S(2)}, u32[]{:S(2)}) collective-permute-start(f32[4,2,64,128]{3,2,1,0:T(8,128)} %get-tuple-element.30), channel_id=1, source_target_pairs={{0,64},{4,452},{8,72},{12,460},{16,80},{20,468},{24,88},{28,476},{... | collective-permute-start | bytes 786440 | tf_op jit(solution)/shard_map/ppermute | solution.py:176
  47.7 14.2 %collective-permute-start.5 = (f32[4,2,64,128]{3,2,1,0:T(8,128)}, f32[4,2,64,128]{3,2,1,0:T(8,128)S(1)}, u32[]{:S(2)}, u32[]{:S(2)}) collective-permute-start(f32[4,2,64,128]{3,2,1,0:T(8,128)} %get-tuple-element.31), channel_id=1, source_target_pairs={{0,32},{32,64},{64,96},{96,128},{128,160},{160,192},{192,224},{224... | collective-permute-start | bytes 786440 | tf_op jit(solution)/shard_map/ppermute | solution.py:166
  52.3 9.6 %collective-permute-start.6 = (f32[4,2,64,128]{3,2,1,0:T(8,128)}, f32[4,2,64,128]{3,2,1,0:T(8,128)S(1)}, u32[]{:S(2)}, u32[]{:S(2)}) collective-permute-start(f32[4,2,64,128]{3,2,1,0:T(8,128)} %get-tuple-element.32), channel_id=1, source_target_pairs={{0,480},{32,0},{64,32},{96,64},{128,96},{160,128},{192,160},{224,1... | collective-permute-start | bytes 786440 | tf_op jit(solution)/shard_map/ppermute | solution.py:166
  54.2 27.0 %collective-permute-start.7 = (bf16[32,64,128]{2,1,0:T(8,128)(2,1)S(1)}, bf16[32,64,128]{2,1,0:T(8,128)(2,1)S(1)}, u32[]{:S(2)}, u32[]{:S(2)}) collective-permute-start(bf16[32,64,128]{2,1,0:T(8,128)(2,1)S(1)} %bitcast.29), channel_id=1, source_target_pairs={{1,0},{2,1},{3,2},{5,4},{6,5},{7,6},{9,8},{10,9},{11,10},{13,12},{... | collective-permute-start | bytes 1572872 | tf_op jit(solution)/shard_map/ppermute | solution.py:161
  56.7 24.6 %collective-permute-start.2 = (bf16[32,64,128]{2,1,0:T(8,128)(2,1)S(1)}, bf16[32,64,128]{2,1,0:T(8,128)(2,1)S(1)}, u32[]{:S(2)}, u32[]{:S(2)}) collective-permute-start(bf16[32,64,128]{2,1,0:T(8,128)(2,1)S(1)} %bitcast.30), channel_id=1, source_target_pairs={{0,1},{1,2},{2,3},{4,5},{5,6},{6,7},{8,9},{9,10},{10,11},{12,13},{... | collective-permute-start | bytes 1572872 | tf_op jit(solution)/shard_map/ppermute | solution.py:161
  61.2 0.7 copy-start
  62.7 9.6 %copy-start.1 = (f32[448,128]{1,0:T(8,128)S(1)}, f32[448,128]{1,0:T(8,128)}, u32[]{:S(2)}) copy-start(f32[448,128]{1,0:T(8,128)} %copy-done) | copy-start | bytes 688132
  62.7 18.6 %copy-start.3 = (bf16[3,3,3,32,64]{4,3,2,1,0:T(8,128)(2,1)S(1)}, bf16[3,3,3,32,64]{4,3,2,1,0:T(8,128)(2,1)}, u32[]{:S(2)}) copy-start(bf16[3,3,3,32,64]{4,3,2,1,0:T(8,128)(2,1)} %weights.3) | copy-start | bytes 331780
  62.7 30.8 %all-to-all-start.1 = ((f32[4,2,64,128]{3,2,1,0:T(8,128)}), f32[4,2,64,128]{3,2,1,0:T(8,128)S(1)}, u32[]{:S(2)}, u32[]{:S(2)}) async-start(f32[4,2,64,128]{3,2,1,0:T(8,128)} %shard_map.60), calls=%async_computation.1 | async-start | bytes 524288 | tf_op jit(solution)/shard_map/all_to_all | solution.py:180
  72.2 9.0 %collective-permute-start.3 = (f32[448,128]{1,0:T(8,128)S(1)}, f32[448,128]{1,0:T(8,128)S(1)}, u32[]{:S(2)}, u32[]{:S(2)}) collective-permute-start(f32[448,128]{1,0:T(8,128)S(1)} %copy-done.1), channel_id=1, source_target_pairs={{0,1},{1,0},{2,3},{3,2},{4,5},{5,4},{6,7},{7,6},{8,9},{9,8},{10,11... | collective-permute-start | bytes 688136 | tf_op jit(solution)/shard_map/ppermute | solution.py:240
  83.3 5.1 %collective-permute-start.8 = (f32[4,4,32,128]{3,2,1,0:T(8,128)S(1)}, f32[4,4,32,128]{3,2,1,0:T(8,128)S(1)}, u32[]{:S(2)}, u32[]{:S(2)}) collective-permute-start(f32[4,4,32,128]{3,2,1,0:T(8,128)S(1)} %get-tuple-element.36), channel_id=1, source_target_pairs={{0,4},{4,0},{8,12},{12,8},{16,20},{20,16},{24,28},{28,24},{1,5},{5... | collective-permute-start | bytes 786440 | tf_op jit(solution)/shard_map/ppermute | solution.py:265
  85.3 12.1 %collective-permute-start.9 = (f32[448,128]{1,0:T(8,128)S(1)}, f32[448,128]{1,0:T(8,128)S(1)}, u32[]{:S(2)}, u32[]{:S(2)}) collective-permute-start(f32[448,128]{1,0:T(8,128)S(1)} %add.3.near), channel_id=1, source_target_pairs={{0,3},{1,2},{2,1},{3,0},{4,7},{5,6},{6,5},{7,4},{8,11},{9,10},{10,... | collective-permute-start | bytes 688136 | tf_op jit(solution)/shard_map/ppermute | solution.py:268
  93.5 10.5 %all-to-all-start.2 = ((f32[16,32,128]{2,1,0:T(8,128)}), f32[16,32,128]{2,1,0:T(8,128)S(1)}, u32[]{:S(2)}, u32[]{:S(2)}) async-start(f32[16,32,128]{2,1,0:T(8,128)} %bitcast.14), calls=%async_computation.2 | async-start | bytes 524288 | tf_op jit(solution)/shard_map/all_to_all | solution.py:180

commit v4 on v3

--- a/solution.py
+++ b/solution.py
@@ -73,8 +73,9 @@
     out[...] = (own[...] + far[...]) + (ahead[...] + behind[...])
 
 
-def pair_sum_kernel(kept, came, out):
-    out[...] = kept[...] + came[...]
+def split_sum_kernel(kept, came, mine, far, ahead, behind):
+    for slot, part in enumerate((mine, ahead, far, behind)):
+        part[...] = kept[slot] + came[slot]
 
 
 def backward_kernel(place, low, mid, high, weights, kept, handed, stacked, product):
@@ -95,11 +96,12 @@
     product[:, :width] = edge
     product[:, -width:] = edge
     chips, share = kept.shape[:2]
-    core = lax.rem(place[0], 2)
+    chip, core = lax.div(place[0], 2), lax.rem(place[0], 2)
     for part, at_core in ((kept, core), (handed, 1 - core)):
-        for chip in range(chips):
+        for slot in range(chips):
+            at_chip = lax.rem(chip + slot, chips)
             for e in range(share):
-                part[chip, e] = row_total(product, cin, (chip * 2 + at_core) * share + e, width)
+                part[slot, e] = row_total(product, cin, (at_chip * 2 + at_core) * share + e, width)
 
 
 def kernel_grad_kernel(planes, grad, out, stacked, shifted_grad):
@@ -194,7 +196,6 @@
 
     x_low, x_high = halos(x_own, "sp")
     g_copies = jnp.broadcast_to(g_own[None], (ring,) + g_own.shape)
-    g_copies, x_low, x_high = lax.optimization_barrier((g_copies, x_low, x_high))
     g_mid = exchange(g_copies, "cin").reshape((-1,) + g_own.shape[1:])
     x_all = lax.all_gather(jnp.stack([x_low, x_own, x_high]), "cout", axis=0)
     rows = x_all.shape[0] * x_all.shape[2]
@@ -210,7 +211,7 @@
             pltpu.VMEM((9 * cin, voxels), BF16),
             pltpu.VMEM((3 * cout, voxels + 2 * width), F32),
         ],
-        flops,
+        40 * flops,
         place,
         x_all,
         weights,
@@ -231,7 +232,7 @@
         sum_kernel,
         piece,
         [],
-        4 * math.prod(piece.shape),
+        40 * flops,
         own,
         around_by_core(far),
         around(ahead, "cin", 1),
@@ -239,7 +240,6 @@
     )
     near_grad = lax.ppermute(local_grad, "sp", [(i, i ^ 1) for i in range(depth)])
     near_sum, g_mid = lax.optimization_barrier((near_sum, g_mid))
-    near_grad, g_mid = lax.optimization_barrier((near_grad, g_mid))
     out_parts = exchange(near_sum, "cin", apart)
 
     cores = 2
@@ -255,7 +255,7 @@
             pltpu.VMEM((9 * cout, voxels), BF16),
             pltpu.VMEM((3 * cin, voxels + 2 * width), F32),
         ],
-        flops,
+        40 * flops,
         place,
         g_low,
         g_mid,
@@ -263,14 +263,26 @@
         weights,
     )
     came = lax.ppermute(handed, "cout", [(i, i ^ 1) for i in range(chips * cores)])
-    pair_dx = call(pair_sum_kernel, chunks, [], math.prod(chunks.shape), kept, came)
     pair_grad = local_grad + near_grad
     far_grad = lax.ppermute(pair_grad, "sp", [(i, depth - 1 - i) for i in range(depth)])
-    pair_dx, out_parts = lax.optimization_barrier((pair_dx, out_parts))
-    same_core = [[cores * y + core for y in range(chips)] for core in range(cores)]
-    dx_parts = exchange(
-        pair_dx.reshape((chips * share, cin, width)), "cout", same_core
-    ).reshape(chunks.shape)
+    mine, far, ahead, behind = call(
+        split_sum_kernel, (chunk, chunk, chunk, chunk), [], math.prod(chunks.shape), kept, came
+    )
+
+    def chip_step(block, step):
+        count = chips * cores
+        return lax.ppermute(block, "cout", [(i, (i + cores * step) % count) for i in range(count)])
+
+    dx_total = call(
+        sum_kernel,
+        chunk,
+        [],
+        4 * math.prod(chunk.shape),
+        mine,
+        chip_step(far, 2),
+        chip_step(ahead, 1),
+        chip_step(behind, -1),
+    )
 
     scale = 1.0 / math.sqrt(depth * voxels)
     weight_grad = call(
@@ -286,7 +298,7 @@
         return jnp.transpose(summed, (1, 0, 2)).astype(BF16).reshape(like.shape)
 
     out_total = jnp.sum(out_parts, axis=0)
-    return placed_as(out_total, out_grad), placed_as(jnp.sum(dx_parts, axis=0), activations), weight_grad
+    return placed_as(out_total, out_grad), placed_as(dx_total, activations), weight_grad
 
 
 def solution(mesh):

time: 105 us -> 96.8 us (0.922)
  the two profiles are of different devices: /device:TPU:34 before, /device:TPU:24 now
where the time goes in v4:
time: 96.8 us; the launch traced here: 96 us
  starting transfers between devices  67 us (69%)
  blocking collectives  13.6 us (14%)
  Pallas kernels  7.98 us (8%)
  local copies, waits for them, and re-layouts  3.7 us (4%)
  waiting for transfers between devices  2.81 us (3%)
    all_to_all x2, starting transfers between devices, exchange(): lax.all_to_all(blocks, axis, 0, 0, tiled=True, axis_index_groups=groups)  25 us
    all_gather x1, blocking collectives, body(): x_all = lax.all_gather(jnp.stack([x_low, x_own, x_high]), 'cout', axis=0)  13.6 us
    ppermute x3, starting transfers between devices, chip_step(): lax.ppermute(block, 'cout', [(i, (i + cores * step) % count) for i in ran...  9.21 us
    ppermute x2, starting transfers between devices, halos(): lax.ppermute(plane, axis, forward)  8.43 us
    pallas_call x7, Pallas kernels, call(): pl.pallas_call(kernel, out_shape=out, in_specs=specs, scratch_shapes=scra...  7.98 us
    ppermute x2, starting transfers between devices, around(): lax.ppermute(block, axis, [(i, (i + step) % count) for i in range(count)])  7.06 us
    ppermute x1, starting transfers between devices, around_by_core(): return lax.ppermute(block, ('cin', 'cout'), pairs)  4.73 us
    ppermute x1, starting transfers between devices, body(): lax.ppermute(pair_grad, 'sp', [(i, depth - 1 - i) for i in range(depth)])  4.04 us
  transfers between devices with their start and end apart: 15, of which 2 were waited for; matrix products, arithmetic and copies ran while one was open for 2% of the time, Pallas kernels for 8%

profile of v4, /device:TPU:24, one launch (start us, length us, event | category | flops | bytes accessed | tf_op | source)
XLA Modules:
  0.0 96.0 jit_solution(7706230939474443028)
XLA Ops:
  0.6 0.0 copy-start.4
  0.6 0.8 copy.15
  1.4 3.4 %collective-permute-start = (bf16[4,32,128]{2,1,0:T(8,128)(2,1)S(1)}, bf16[4,32,128]{2,1,0:T(8,128)(2,1)S(1)}, u32[]{:S(2)}, u32[]{:S(2)}) collective-permute-start(bf16[4,32,128]{2,1,0:T(8,128)(2,1)S(1)} %bitcast.33), channel_id=1, source_target_pairs={{0,1},{1,2},{2,3},{4,5},{5,6},{6,7},{8,9},{9,10},{10,11},{12,13},{... | collective-permute-start | bytes 98312 | tf_op jit(solution)/shard_map/ppermute | solution.py:163
  4.8 1.3 %collective-permute-start.1 = (bf16[4,32,128]{2,1,0:T(8,128)(2,1)S(1)}, bf16[4,32,128]{2,1,0:T(8,128)(2,1)S(1)}, u32[]{:S(2)}, u32[]{:S(2)}) collective-permute-start(bf16[4,32,128]{2,1,0:T(8,128)(2,1)S(1)} %bitcast.34), channel_id=1, source_target_pairs={{1,0},{2,1},{3,2},{5,4},{6,5},{7,6},{9,8},{10,9},{11,10},{13,12},{... | collective-permute-start | bytes 98312 | tf_op jit(solution)/shard_map/ppermute | solution.py:163
  6.1 0.0 copy-done.4
  6.1 0.9 broadcast_in_dim.2
  7.1 15.2 %all-to-all-start = ((bf16[16,2,64,128]{3,2,1,0:T(8,128)(2,1)}), bf16[16,2,64,128]{3,2,1,0:T(8,128)(2,1)S(1)}, u32[]{:S(2)}, u32[]{:S(2)}) async-start(bf16[16,2,64,128]{3,2,1,0:T(8,128)(2,1)} %broadcast_in_dim.2), calls=%async_computation | async-start | bytes 1048576 | tf_op jit(solution)/shard_map/all_to_all | solution.py:182
  22.3 0.0 collective-permute-done
  22.3 0.0 collective-permute-done.1
  22.3 0.0 copy-start
  22.3 13.6 %all-gather = bf16[24,4,32,128]{3,2,1,0:T(8,128)(2,1)S(1)} all-gather(bf16[3,4,32,128]{3,2,1,0:T(8,128)(2,1)S(1)} %pad_maximum_fusion), channel_id=2, replica_groups=mesh['cin'=16,'cout'=8,'sp'=4] {'cout'}, dimensions={0}, use_global_device_ids=true | all-gather | bytes 884736 | tf_op jit(solution)/shard_map/all_gather | solution.py:200
  35.9 0.0 copy-done
  35.9 2.3 %shard_map.58 = (f32[4,2,64,128]{3,2,1,0:T(8,128)S(1)}, f32[4,2,64,128]{3,2,1,0:T(8,128)S(1)}, f32[4,2,64,128]{3,2,1,0:T(8,128)}, f32[4,2,64,128]{3,2,1,0:T(8,128)S(1)}) custom-call(s32[1]{0:T(128)} %bitcast.10.place, bf16[8,3,4,32,128]{4,3,2,1,0:T(8,128)(2,1)S(1)} %bitcast.26, bf16[3,3,3,32,64]{4,3,2,1,0:T(8,128)(2,1)S(1)} %copy-done), custom_call_target="tpu_custom_call" | custom-call | flops 18119393280 | bytes 897028 | tf_op jit(solution)/shard_map/pallas_call | solution.py:149
  38.3 0.0 copy-start.2
  38.3 0.7 copy-done.2
  38.9 4.7 %collective-permute-start.2 = (f32[4,2,64,128]{3,2,1,0:T(8,128)}, f32[4,2,64,128]{3,2,1,0:T(8,128)S(1)}, u32[]{:S(2)}, u32[]{:S(2)}) collective-permute-start(f32[4,2,64,128]{3,2,1,0:T(8,128)} %get-tuple-element.23), channel_id=1, source_target_pairs={{0,64},{4,452},{8,72},{12,460},{16,80},{20,468},{24,88},{28,476},{... | collective-permute-start | bytes 786440 | tf_op jit(solution)/shard_map/ppermute | solution.py:178
  43.7 3.4 %collective-permute-start.3 = (f32[4,2,64,128]{3,2,1,0:T(8,128)S(1)}, f32[4,2,64,128]{3,2,1,0:T(8,128)}, u32[]{:S(2)}, u32[]{:S(2)}) collective-permute-start(f32[4,2,64,128]{3,2,1,0:T(8,128)S(1)} %get-tuple-element.24), channel_id=1, source_target_pairs={{0,32},{32,64},{64,96},{96,128},{128,160},{160,192},{192,224},{224... | collective-permute-start | bytes 786440 | tf_op jit(solution)/shard_map/ppermute | solution.py:168
  47.1 3.7 %collective-permute-start.4 = (f32[4,2,64,128]{3,2,1,0:T(8,128)S(1)}, f32[4,2,64,128]{3,2,1,0:T(8,128)}, u32[]{:S(2)}, u32[]{:S(2)}) collective-permute-start(f32[4,2,64,128]{3,2,1,0:T(8,128)S(1)} %get-tuple-element.25), channel_id=1, source_target_pairs={{0,480},{32,0},{64,32},{96,64},{128,96},{160,128},{192,160},{224,1... | collective-permute-start | bytes 786440 | tf_op jit(solution)/shard_map/ppermute | solution.py:168
  50.8 0.2 all-to-all-done
  51.0 1.4 %collective-permute-start.6 = (bf16[32,64,128]{2,1,0:T(8,128)(2,1)S(1)}, bf16[32,64,128]{2,1,0:T(8,128)(2,1)S(1)}, u32[]{:S(2)}, u32[]{:S(2)}) collective-permute-start(bf16[32,64,128]{2,1,0:T(8,128)(2,1)S(1)} %bitcast.28), channel_id=1, source_target_pairs={{1,0},{2,1},{3,2},{5,4},{6,5},{7,6},{9,8},{10,9},{11,10},{13,12},{... | collective-permute-start | bytes 1572872 | tf_op jit(solution)/shard_map/ppermute | solution.py:163
  52.4 5.0 %collective-permute-start.5 = (bf16[32,64,128]{2,1,0:T(8,128)(2,1)S(1)}, bf16[32,64,128]{2,1,0:T(8,128)(2,1)S(1)}, u32[]{:S(2)}, u32[]{:S(2)}) collective-permute-start(bf16[32,64,128]{2,1,0:T(8,128)(2,1)S(1)} %bitcast.29), channel_id=1, source_target_pairs={{0,1},{1,2},{2,3},{4,5},{5,6},{6,7},{8,9},{9,10},{10,11},{12,13},{... | collective-permute-start | bytes 1572872 | tf_op jit(solution)/shard_map/ppermute | solution.py:163
  57.4 1.1 %shard_map.59 = f32[448,128]{1,0:T(8,128)S(1)} custom-call(bf16[8,3,4,32,128]{4,3,2,1,0:T(8,128)(2,1)S(1)} %bitcast.27, bf16[32,64,128]{2,1,0:T(8,128)(2,1)S(1)} %bitcast.30), custom_call_target="tpu_custom_call" | custom-call | flops 452984832 | bytes 1310720 | tf_op jit(solution)/shard_map/pallas_call | solution.py:149
  58.5 0.0 collective-permute-done.2.far
  58.5 3.9 %collective-permute-start.11 = (f32[448,128]{1,0:T(8,128)S(1)}, f32[448,128]{1,0:T(8,128)S(1)}, u32[]{:S(2)}, u32[]{:S(2)}) collective-permute-start(f32[448,128]{1,0:T(8,128)S(1)} %shard_map.59), channel_id=1, source_target_pairs={{0,1},{1,0},{2,3},{3,2},{4,5},{5,4},{6,7},{7,6},{8,9},{9,8},{10,11... | collective-permute-start | bytes 688136 | tf_op jit(solution)/shard_map/ppermute | solution.py:241
  62.4 0.0 collective-permute-done.3.ahead
  62.4 0.0 collective-permute-done.4.behind
  62.5 0.0 copy-done.3
  62.5 1.8 %shard_map.60 = f32[4,2,64,128]{3,2,1,0:T(8,128)} custom-call(f32[4,2,64,128]{3,2,1,0:T(8,128)S(1)} %copy-done.3, f32[4,2,64,128]{3,2,1,0:T(8,128)S(1)} %collective-permute-done.2.far, f32[4,2,64,128]{3,2,1,0:T(8,128)} %collective-permute-done.3.ahead, f32[4,2,64,128]{3,2,1,0:T(8,128)} %collective-permute-done.4.behind), custom_call_target="tpu_custom_call" | custom-call | flops 18119393280 | bytes 1048576 | tf_op jit(solution)/shard_map/pallas_call | solution.py:149
  64.2 9.8 %all-to-all-start.1 = ((f32[4,2,64,128]{3,2,1,0:T(8,128)}), f32[4,2,64,128]{3,2,1,0:T(8,128)S(1)}, u32[]{:S(2)}, u32[]{:S(2)}) async-start(f32[4,2,64,128]{3,2,1,0:T(8,128)} %shard_map.60), calls=%async_computation.1 | async-start | bytes 524288 | tf_op jit(solution)/shard_map/all_to_all | solution.py:182
  74.0 0.0 collective-permute-done.6.high
  74.0 0.0 collective-permute-done.5.low
  74.0 0.0 copy-done.1
  74.0 1.9 %shard_map.61 = (f32[4,4,32,128]{3,2,1,0:T(8,128)S(1)}, f32[4,4,32,128]{3,2,1,0:T(8,128)S(1)}) custom-call(s32[1]{0:T(128)} %bitcast.13.place, bf16[32,64,128]{2,1,0:T(8,128)(2,1)S(1)} %collective-permute-done.5.low, bf16[32,64,128]{2,1,0:T(8,128)(2,1)S(1)} %bitcast.31, bf16[32,64,128]{2,1,0:T(8,128)(2,1)S(1)} %collective-permute-done.6.high, ...), custom_call_target="tpu_custom_call" | custom-call | flops 18119393280 | bytes 1683460 | tf_op jit(solution)/shard_map/pallas_call | solution.py:149
  76.0 1.9 %collective-permute-start.7 = (f32[4,4,32,128]{3,2,1,0:T(8,128)S(1)}, f32[4,4,32,128]{3,2,1,0:T(8,128)S(1)}, u32[]{:S(2)}, u32[]{:S(2)}) collective-permute-start(f32[4,4,32,128]{3,2,1,0:T(8,128)S(1)} %get-tuple-element.29), channel_id=1, source_target_pairs={{0,4},{4,0},{8,12},{12,8},{16,20},{20,16},{24,28},{28,24},{1,5},{5... | collective-permute-start | bytes 786440 | tf_op jit(solution)/shard_map/ppermute | solution.py:265
  77.9 0.0 collective-permute-done.11
  77.9 4.0 %collective-permute-start.12 = (f32[448,128]{1,0:T(8,128)S(1)}, f32[448,128]{1,0:T(8,128)S(1)}, u32[]{:S(2)}, u32[]{:S(2)}) collective-permute-start(f32[448,128]{1,0:T(8,128)S(1)} %add.3.near), channel_id=1, source_target_pairs={{0,3},{1,2},{2,1},{3,0},{4,7},{5,6},{6,5},{7,4},{8,11},{9,10},{10,... | collective-permute-start | bytes 688136 | tf_op jit(solution)/shard_map/ppermute | solution.py:267
  82.0 0.0 collective-permute-done.7.came
  82.0 3.4 %collective-permute-start.8 = (f32[4,32,128]{2,1,0:T(8,128)S(1)}, f32[4,32,128]{2,1,0:T(8,128)S(1)}, u32[]{:S(2)}, u32[]{:S(2)}) collective-permute-start(f32[4,32,128]{2,1,0:T(8,128)S(1)} %get-tuple-element.31), channel_id=1, source_target_pairs={{0,16},{4,20},{8,24},{12,28},{16,0},{20,4},{24,8},{28,12},{1,17},{... | collective-permute-start | bytes 196616 | tf_op jit(solution)/shard_map/ppermute | solution.py:274
  85.4 2.6 %collective-permute-start.9 = (f32[4,32,128]{2,1,0:T(8,128)S(1)}, f32[4,32,128]{2,1,0:T(8,128)S(1)}, u32[]{:S(2)}, u32[]{:S(2)}) collective-permute-start(f32[4,32,128]{2,1,0:T(8,128)S(1)} %get-tuple-element.32), channel_id=1, source_target_pairs={{0,8},{4,12},{8,16},{12,20},{16,24},{20,28},{24,0},{28,4},{1,9},{5... | collective-permute-start | bytes 196616 | tf_op jit(solution)/shard_map/ppermute | solution.py:274
  88.0 3.3 %collective-permute-start.10 = (f32[4,32,128]{2,1,0:T(8,128)S(1)}, f32[4,32,128]{2,1,0:T(8,128)S(1)}, u32[]{:S(2)}, u32[]{:S(2)}) collective-permute-start(f32[4,32,128]{2,1,0:T(8,128)S(1)} %get-tuple-element.33), channel_id=1, source_target_pairs={{0,24},{4,28},{8,0},{12,4},{16,8},{20,12},{24,16},{28,20},{1,25},{... | collective-permute-start | bytes 196616 | tf_op jit(solution)/shard_map/ppermute | solution.py:274
  91.3 0.0 collective-permute-done.12.far
  91.3 0.8 shard_map.64
  92.1 0.0 all-to-all-done.1
  92.1 0.6 copy.11
  92.8 0.0 collective-permute-done.8.far
  92.8 0.0 collective-permute-done.9.ahead
  92.8 2.6 %collective-permute-done.10.behind = f32[4,32,128]{2,1,0:T(8,128)S(1)} collective-permute-done((f32[4,32,128]{2,1,0:T(8,128)S(1)}, f32[4,32,128]{2,1,0:T(8,128)S(1)}, u32[]{:S(2)}, u32[]{:S(2)}) %collective-permute-start.10) | collective-permute-done | bytes 65568 | tf_op jit(solution)/shard_map/ppermute | solution.py:274
  95.4 0.6 copy.12
  (9 shorter events, 0.1 us)
Async XLA Ops:
  0.6 5.5 %copy-start.4 = (bf16[64,1,2,128]{3,2,1,0:T(2,128)(2,1)S(1)}, bf16[64,1,2,128]{3,2,1,0:T(2,128)(2,1)}, u32[]{:S(2)}) copy-start(bf16[64,1,2,128]{3,2,1,0:T(2,128)(2,1)} %param.5) | copy-start | bytes 98308
  1.4 20.9 %collective-permute-start = (bf16[4,32,128]{2,1,0:T(8,128)(2,1)S(1)}, bf16[4,32,128]{2,1,0:T(8,128)(2,1)S(1)}, u32[]{:S(2)}, u32[]{:S(2)}) collective-permute-start(bf16[4,32,128]{2,1,0:T(8,128)(2,1)S(1)} %bitcast.33), channel_id=1, source_target_pairs={{0,1},{1,2},{2,3},{4,5},{5,6},{6,7},{8,9},{9,10},{10,11},{12,13},{... | collective-permute-start | bytes 98312 | tf_op jit(solution)/shard_map/ppermute | solution.py:163
  4.8 17.5 %collective-permute-start.1 = (bf16[4,32,128]{2,1,0:T(8,128)(2,1)S(1)}, bf16[4,32,128]{2,1,0:T(8,128)(2,1)S(1)}, u32[]{:S(2)}, u32[]{:S(2)}) collective-permute-start(bf16[4,32,128]{2,1,0:T(8,128)(2,1)S(1)} %bitcast.34), channel_id=1, source_target_pairs={{1,0},{2,1},{3,2},{5,4},{6,5},{7,6},{9,8},{10,9},{11,10},{13,12},{... | collective-permute-start | bytes 98312 | tf_op jit(solution)/shard_map/ppermute | solution.py:163
  7.1 43.9 %all-to-all-start = ((bf16[16,2,64,128]{3,2,1,0:T(8,128)(2,1)}), bf16[16,2,64,128]{3,2,1,0:T(8,128)(2,1)S(1)}, u32[]{:S(2)}, u32[]{:S(2)}) async-start(bf16[16,2,64,128]{3,2,1,0:T(8,128)(2,1)} %broadcast_in_dim.2), calls=%async_computation | async-start | bytes 1048576 | tf_op jit(solution)/shard_map/all_to_all | solution.py:182
  22.3 13.6 %copy-start = (bf16[3,3,3,32,64]{4,3,2,1,0:T(8,128)(2,1)S(1)}, bf16[3,3,3,32,64]{4,3,2,1,0:T(8,128)(2,1)}, u32[]{:S(2)}) copy-start(bf16[3,3,3,32,64]{4,3,2,1,0:T(8,128)(2,1)} %weights.3) | copy-start | bytes 331780
  38.3 0.7 copy-start.2
  38.9 19.6 %collective-permute-start.2 = (f32[4,2,64,128]{3,2,1,0:T(8,128)}, f32[4,2,64,128]{3,2,1,0:T(8,128)S(1)}, u32[]{:S(2)}, u32[]{:S(2)}) collective-permute-start(f32[4,2,64,128]{3,2,1,0:T(8,128)} %get-tuple-element.23), channel_id=1, source_target_pairs={{0,64},{4,452},{8,72},{12,460},{16,80},{20,468},{24,88},{28,476},{... | collective-permute-start | bytes 786440 | tf_op jit(solution)/shard_map/ppermute | solution.py:178
  43.7 18.7 %collective-permute-start.3 = (f32[4,2,64,128]{3,2,1,0:T(8,128)S(1)}, f32[4,2,64,128]{3,2,1,0:T(8,128)}, u32[]{:S(2)}, u32[]{:S(2)}) collective-permute-start(f32[4,2,64,128]{3,2,1,0:T(8,128)S(1)} %get-tuple-element.24), channel_id=1, source_target_pairs={{0,32},{32,64},{64,96},{96,128},{128,160},{160,192},{192,224},{224... | collective-permute-start | bytes 786440 | tf_op jit(solution)/shard_map/ppermute | solution.py:168
  47.1 15.3 %collective-permute-start.4 = (f32[4,2,64,128]{3,2,1,0:T(8,128)S(1)}, f32[4,2,64,128]{3,2,1,0:T(8,128)}, u32[]{:S(2)}, u32[]{:S(2)}) collective-permute-start(f32[4,2,64,128]{3,2,1,0:T(8,128)S(1)} %get-tuple-element.25), channel_id=1, source_target_pairs={{0,480},{32,0},{64,32},{96,64},{128,96},{160,128},{192,160},{224,1... | collective-permute-start | bytes 786440 | tf_op jit(solution)/shard_map/ppermute | solution.py:168
  51.0 11.5 %copy-start.3 = (f32[4,2,64,128]{3,2,1,0:T(8,128)S(1)}, f32[4,2,64,128]{3,2,1,0:T(8,128)}, u32[]{:S(2)}) copy-start(f32[4,2,64,128]{3,2,1,0:T(8,128)} %copy-done.2) | copy-start | bytes 786436
  51.0 23.1 %collective-permute-start.6 = (bf16[32,64,128]{2,1,0:T(8,128)(2,1)S(1)}, bf16[32,64,128]{2,1,0:T(8,128)(2,1)S(1)}, u32[]{:S(2)}, u32[]{:S(2)}) collective-permute-start(bf16[32,64,128]{2,1,0:T(8,128)(2,1)S(1)} %bitcast.28), channel_id=1, source_target_pairs={{1,0},{2,1},{3,2},{5,4},{6,5},{7,6},{9,8},{10,9},{11,10},{13,12},{... | collective-permute-start | bytes 1572872 | tf_op jit(solution)/shard_map/ppermute | solution.py:163
  52.4 21.7 %collective-permute-start.5 = (bf16[32,64,128]{2,1,0:T(8,128)(2,1)S(1)}, bf16[32,64,128]{2,1,0:T(8,128)(2,1)S(1)}, u32[]{:S(2)}, u32[]{:S(2)}) collective-permute-start(bf16[32,64,128]{2,1,0:T(8,128)(2,1)S(1)} %bitcast.29), channel_id=1, source_target_pairs={{0,1},{1,2},{2,3},{4,5},{5,6},{6,7},{8,9},{9,10},{10,11},{12,13},{... | collective-permute-start | bytes 1572872 | tf_op jit(solution)/shard_map/ppermute | solution.py:163
  58.5 19.4 %collective-permute-start.11 = (f32[448,128]{1,0:T(8,128)S(1)}, f32[448,128]{1,0:T(8,128)S(1)}, u32[]{:S(2)}, u32[]{:S(2)}) collective-permute-start(f32[448,128]{1,0:T(8,128)S(1)} %shard_map.59), channel_id=1, source_target_pairs={{0,1},{1,0},{2,3},{3,2},{4,5},{5,4},{6,7},{7,6},{8,9},{9,8},{10,11... | collective-permute-start | bytes 688136 | tf_op jit(solution)/shard_map/ppermute | solution.py:241
  64.2 9.8 %copy-start.1 = (bf16[3,3,3,32,64]{4,3,2,1,0:T(8,128)(2,1)S(1)}, bf16[3,3,3,32,64]{4,3,2,1,0:T(8,128)(2,1)}, u32[]{:S(2)}) copy-start(bf16[3,3,3,32,64]{4,3,2,1,0:T(8,128)(2,1)} %weights.3) | copy-start | bytes 331780
  64.2 27.9 %all-to-all-start.1 = ((f32[4,2,64,128]{3,2,1,0:T(8,128)}), f32[4,2,64,128]{3,2,1,0:T(8,128)S(1)}, u32[]{:S(2)}, u32[]{:S(2)}) async-start(f32[4,2,64,128]{3,2,1,0:T(8,128)} %shard_map.60), calls=%async_computation.1 | async-start | bytes 524288 | tf_op jit(solution)/shard_map/all_to_all | solution.py:182
  76.0 6.0 %collective-permute-start.7 = (f32[4,4,32,128]{3,2,1,0:T(8,128)S(1)}, f32[4,4,32,128]{3,2,1,0:T(8,128)S(1)}, u32[]{:S(2)}, u32[]{:S(2)}) collective-permute-start(f32[4,4,32,128]{3,2,1,0:T(8,128)S(1)} %get-tuple-element.29), channel_id=1, source_target_pairs={{0,4},{4,0},{8,12},{12,8},{16,20},{20,16},{24,28},{28,24},{1,5},{5... | collective-permute-start | bytes 786440 | tf_op jit(solution)/shard_map/ppermute | solution.py:265
  77.9 13.3 %collective-permute-start.12 = (f32[448,128]{1,0:T(8,128)S(1)}, f32[448,128]{1,0:T(8,128)S(1)}, u32[]{:S(2)}, u32[]{:S(2)}) collective-permute-start(f32[448,128]{1,0:T(8,128)S(1)} %add.3.near), channel_id=1, source_target_pairs={{0,3},{1,2},{2,1},{3,0},{4,7},{5,6},{6,5},{7,4},{8,11},{9,10},{10,... | collective-permute-start | bytes 688136 | tf_op jit(solution)/shard_map/ppermute | solution.py:267
  82.0 10.7 %collective-permute-start.8 = (f32[4,32,128]{2,1,0:T(8,128)S(1)}, f32[4,32,128]{2,1,0:T(8,128)S(1)}, u32[]{:S(2)}, u32[]{:S(2)}) collective-permute-start(f32[4,32,128]{2,1,0:T(8,128)S(1)} %get-tuple-element.31), channel_id=1, source_target_pairs={{0,16},{4,20},{8,24},{12,28},{16,0},{20,4},{24,8},{28,12},{1,17},{... | collective-permute-start | bytes 196616 | tf_op jit(solution)/shard_map/ppermute | solution.py:274
  85.4 7.4 %collective-permute-start.9 = (f32[4,32,128]{2,1,0:T(8,128)S(1)}, f32[4,32,128]{2,1,0:T(8,128)S(1)}, u32[]{:S(2)}, u32[]{:S(2)}) collective-permute-start(f32[4,32,128]{2,1,0:T(8,128)S(1)} %get-tuple-element.32), channel_id=1, source_target_pairs={{0,8},{4,12},{8,16},{12,20},{16,24},{20,28},{24,0},{28,4},{1,9},{5... | collective-permute-start | bytes 196616 | tf_op jit(solution)/shard_map/ppermute | solution.py:274
  88.0 7.4 %collective-permute-start.10 = (f32[4,32,128]{2,1,0:T(8,128)S(1)}, f32[4,32,128]{2,1,0:T(8,128)S(1)}, u32[]{:S(2)}, u32[]{:S(2)}) collective-permute-start(f32[4,32,128]{2,1,0:T(8,128)S(1)} %get-tuple-element.33), channel_id=1, source_target_pairs={{0,24},{4,28},{8,0},{12,4},{16,8},{20,12},{24,16},{28,20},{1,25},{... | collective-permute-start | bytes 196616 | tf_op jit(solution)/shard_map/ppermute | solution.py:274

commit v5 on v4

--- a/solution.py
+++ b/solution.py
@@ -10,17 +10,17 @@
 
 F32 = jnp.float32
 BF16 = jnp.bfloat16
-VMEM_LIMIT = 40 * 1024 * 1024
+VMEM_LIMIT = 16 * 1024 * 1024
 
 
 def shifted(plane, step):
     if step == 0:
         return plane
     width = plane.shape[-1]
-    moved = pltpu.roll(plane.astype(F32), (-step) % width, plane.ndim - 1)
+    moved = pltpu.roll(plane, (-step) % width, plane.ndim - 1)
     lane = lax.broadcasted_iota(jnp.int32, plane.shape, plane.ndim - 1)
     edge = width - 1 if step > 0 else 0
-    return jnp.where(lane == edge, 0.0, moved).astype(plane.dtype)
+    return jnp.where(lane == edge, jnp.zeros_like(moved), moved)
 
 
 def stack_taps(planes, stacked):
@@ -69,8 +69,8 @@
                 (own, ahead, far, behind)[slot][q, e] = row_total(product, cout, row, width)
 
 
-def sum_kernel(own, far, ahead, behind, out):
-    out[...] = (own[...] + far[...]) + (ahead[...] + behind[...])
+def sum_kernel(first, second, third, fourth, out):
+    out[...] = (first[...] + second[...]) + (third[...] + fourth[...])
 
 
 def split_sum_kernel(kept, came, mine, far, ahead, behind):
@@ -234,9 +234,9 @@
         [],
         40 * flops,
         own,
-        around_by_core(far),
         around(ahead, "cin", 1),
         around(behind, "cin", -1),
+        around_by_core(far),
     )
     near_grad = lax.ppermute(local_grad, "sp", [(i, i ^ 1) for i in range(depth)])
     near_sum, g_mid = lax.optimization_barrier((near_sum, g_mid))

time: 96.8 us -> 96.3 us (level)
  starting transfers between devices: 67 us -> 65.6 us
  waiting for transfers between devices: 2.81 us -> 4.13 us
    all_to_all x2, waiting for transfers between devices: 0.19 us -> 1.43 us  [exchange(): lax.all_to_all(blocks, axis, 0, 0, tiled=True, axis_index_groups=groups)]
    ppermute x1, starting transfers between devices: 4.73 us -> 3.52 us  [around_by_core(): return lax.ppermute(block, ('cin', 'cout'), pairs)]
where the time goes in v5:
time: 96.3 us; the launch traced here: 95.6 us
  starting transfers between devices  65.6 us (68%)
  blocking collectives  13.6 us (14%)
  Pallas kernels  7.57 us (8%)
  waiting for transfers between devices  4.13 us (4%)
  local copies, waits for them, and re-layouts  3.7 us (4%)
    all_to_all x2, starting transfers between devices, exchange(): lax.all_to_all(blocks, axis, 0, 0, tiled=True, axis_index_groups=groups)  24.6 us
    all_gather x1, blocking collectives, body(): x_all = lax.all_gather(jnp.stack([x_low, x_own, x_high]), 'cout', axis=0)  13.6 us
    ppermute x3, starting transfers between devices, chip_step(): lax.ppermute(block, 'cout', [(i, (i + cores * step) % count) for i in ran...  9.19 us
    ppermute x2, starting transfers between devices, halos(): lax.ppermute(plane, axis, forward)  8.18 us
    pallas_call x7, Pallas kernels, call(): pl.pallas_call(kernel, out_shape=out, in_specs=specs, scratch_shapes=scra...  7.57 us
    ppermute x2, starting transfers between devices, around(): lax.ppermute(block, axis, [(i, (i + step) % count) for i in range(count)])  7.06 us
    ppermute x1, starting transfers between devices, body(): lax.ppermute(pair_grad, 'sp', [(i, depth - 1 - i) for i in range(depth)])  4.5 us
    ppermute x1, starting transfers between devices, body(): lax.ppermute(local_grad, 'sp', [(i, i ^ 1) for i in range(depth)])  3.89 us
  transfers between devices with their start and end apart: 15, of which 2 were waited for; matrix products, arithmetic and copies ran while one was open for 2% of the time, Pallas kernels for 8%

profile of v5, /device:TPU:24, one launch (start us, length us, event | category | flops | bytes accessed | tf_op | source)
XLA Modules:
  0.0 95.6 jit_solution(8976752876425439289)
XLA Ops:
  0.6 0.0 copy-start.4
  0.6 0.8 copy.15
  1.4 3.4 %collective-permute-start = (bf16[4,32,128]{2,1,0:T(8,128)(2,1)S(1)}, bf16[4,32,128]{2,1,0:T(8,128)(2,1)S(1)}, u32[]{:S(2)}, u32[]{:S(2)}) collective-permute-start(bf16[4,32,128]{2,1,0:T(8,128)(2,1)S(1)} %bitcast.33), channel_id=1, source_target_pairs={{0,1},{1,2},{2,3},{4,5},{5,6},{6,7},{8,9},{9,10},{10,11},{12,13},{... | collective-permute-start | bytes 98312 | tf_op jit(solution)/shard_map/ppermute | solution.py:163
  4.8 1.3 %collective-permute-start.1 = (bf16[4,32,128]{2,1,0:T(8,128)(2,1)S(1)}, bf16[4,32,128]{2,1,0:T(8,128)(2,1)S(1)}, u32[]{:S(2)}, u32[]{:S(2)}) collective-permute-start(bf16[4,32,128]{2,1,0:T(8,128)(2,1)S(1)} %bitcast.34), channel_id=1, source_target_pairs={{1,0},{2,1},{3,2},{5,4},{6,5},{7,6},{9,8},{10,9},{11,10},{13,12},{... | collective-permute-start | bytes 98312 | tf_op jit(solution)/shard_map/ppermute | solution.py:163
  6.1 0.0 copy-done.4
  6.1 0.9 broadcast_in_dim.2
  7.1 15.2 %all-to-all-start = ((bf16[16,2,64,128]{3,2,1,0:T(8,128)(2,1)}), bf16[16,2,64,128]{3,2,1,0:T(8,128)(2,1)S(1)}, u32[]{:S(2)}, u32[]{:S(2)}) async-start(bf16[16,2,64,128]{3,2,1,0:T(8,128)(2,1)} %broadcast_in_dim.2), calls=%async_computation | async-start | bytes 1048576 | tf_op jit(solution)/shard_map/all_to_all | solution.py:182
  22.3 0.0 collective-permute-done
  22.3 0.0 collective-permute-done.1
  22.3 0.0 copy-start
  22.3 13.6 %all-gather = bf16[24,4,32,128]{3,2,1,0:T(8,128)(2,1)S(1)} all-gather(bf16[3,4,32,128]{3,2,1,0:T(8,128)(2,1)S(1)} %pad_maximum_fusion), channel_id=2, replica_groups=mesh['cin'=16,'cout'=8,'sp'=4] {'cout'}, dimensions={0}, use_global_device_ids=true | all-gather | bytes 884736 | tf_op jit(solution)/shard_map/all_gather | solution.py:200
  35.9 0.0 copy-done
  35.9 2.3 %shard_map.58 = (f32[4,2,64,128]{3,2,1,0:T(8,128)S(1)}, f32[4,2,64,128]{3,2,1,0:T(8,128)}, f32[4,2,64,128]{3,2,1,0:T(8,128)S(1)}, f32[4,2,64,128]{3,2,1,0:T(8,128)S(1)}) custom-call(s32[1]{0:T(128)} %bitcast.10.place, bf16[8,3,4,32,128]{4,3,2,1,0:T(8,128)(2,1)S(1)} %bitcast.26, bf16[3,3,3,32,64]{4,3,2,1,0:T(8,128)(2,1)S(1)} %copy-done), custom_call_target="tpu_custom_call" | custom-call | flops 18119393280 | bytes 897028 | tf_op jit(solution)/shard_map/pallas_call | solution.py:149
  38.2 0.0 copy-start.2
  38.2 0.7 copy-done.2
  38.9 3.8 %collective-permute-start.2 = (f32[4,2,64,128]{3,2,1,0:T(8,128)}, f32[4,2,64,128]{3,2,1,0:T(8,128)S(1)}, u32[]{:S(2)}, u32[]{:S(2)}) collective-permute-start(f32[4,2,64,128]{3,2,1,0:T(8,128)} %get-tuple-element.23), channel_id=1, source_target_pairs={{0,32},{32,64},{64,96},{96,128},{128,160},{160,192},{192,224},{224... | collective-permute-start | bytes 786440 | tf_op jit(solution)/shard_map/ppermute | solution.py:168
  42.7 3.2 %collective-permute-start.3 = (f32[4,2,64,128]{3,2,1,0:T(8,128)S(1)}, f32[4,2,64,128]{3,2,1,0:T(8,128)}, u32[]{:S(2)}, u32[]{:S(2)}) collective-permute-start(f32[4,2,64,128]{3,2,1,0:T(8,128)S(1)} %get-tuple-element.24), channel_id=1, source_target_pairs={{0,480},{32,0},{64,32},{96,64},{128,96},{160,128},{192,160},{224,1... | collective-permute-start | bytes 786440 | tf_op jit(solution)/shard_map/ppermute | solution.py:168
  46.0 3.5 %collective-permute-start.4 = (f32[4,2,64,128]{3,2,1,0:T(8,128)S(1)}, f32[4,2,64,128]{3,2,1,0:T(8,128)}, u32[]{:S(2)}, u32[]{:S(2)}) collective-permute-start(f32[4,2,64,128]{3,2,1,0:T(8,128)S(1)} %get-tuple-element.25), channel_id=1, source_target_pairs={{0,64},{4,452},{8,72},{12,460},{16,80},{20,468},{24,88},{28,476},{... | collective-permute-start | bytes 786440 | tf_op jit(solution)/shard_map/ppermute | solution.py:178
  49.5 1.4 %all-to-all-done = bf16[16,2,64,128]{3,2,1,0:T(8,128)(2,1)S(1)} async-done(((bf16[16,2,64,128]{3,2,1,0:T(8,128)(2,1)}), bf16[16,2,64,128]{3,2,1,0:T(8,128)(2,1)S(1)}, u32[]{:S(2)}, u32[]{:S(2)}) %all-to-all-start) | async-done | bytes 524320 | tf_op jit(solution)/shard_map/all_to_all | solution.py:182
  51.0 1.4 %collective-permute-start.6 = (bf16[32,64,128]{2,1,0:T(8,128)(2,1)S(1)}, bf16[32,64,128]{2,1,0:T(8,128)(2,1)S(1)}, u32[]{:S(2)}, u32[]{:S(2)}) collective-permute-start(bf16[32,64,128]{2,1,0:T(8,128)(2,1)S(1)} %bitcast.28), channel_id=1, source_target_pairs={{1,0},{2,1},{3,2},{5,4},{6,5},{7,6},{9,8},{10,9},{11,10},{13,12},{... | collective-permute-start | bytes 1572872 | tf_op jit(solution)/shard_map/ppermute | solution.py:163
  52.4 4.8 %collective-permute-start.5 = (bf16[32,64,128]{2,1,0:T(8,128)(2,1)S(1)}, bf16[32,64,128]{2,1,0:T(8,128)(2,1)S(1)}, u32[]{:S(2)}, u32[]{:S(2)}) collective-permute-start(bf16[32,64,128]{2,1,0:T(8,128)(2,1)S(1)} %bitcast.29), channel_id=1, source_target_pairs={{0,1},{1,2},{2,3},{4,5},{5,6},{6,7},{8,9},{9,10},{10,11},{12,13},{... | collective-permute-start | bytes 1572872 | tf_op jit(solution)/shard_map/ppermute | solution.py:163
  57.2 1.0 %shard_map.59 = f32[448,128]{1,0:T(8,128)S(1)} custom-call(bf16[8,3,4,32,128]{4,3,2,1,0:T(8,128)(2,1)S(1)} %bitcast.27, bf16[32,64,128]{2,1,0:T(8,128)(2,1)S(1)} %bitcast.30), custom_call_target="tpu_custom_call" | custom-call | flops 452984832 | bytes 1310720 | tf_op jit(solution)/shard_map/pallas_call | solution.py:149
  58.1 0.0 collective-permute-done.2.second
  58.2 3.9 %collective-permute-start.11 = (f32[448,128]{1,0:T(8,128)S(1)}, f32[448,128]{1,0:T(8,128)S(1)}, u32[]{:S(2)}, u32[]{:S(2)}) collective-permute-start(f32[448,128]{1,0:T(8,128)S(1)} %shard_map.59), channel_id=1, source_target_pairs={{0,1},{1,0},{2,3},{3,2},{4,5},{5,4},{6,7},{7,6},{8,9},{9,8},{10,11... | collective-permute-start | bytes 688136 | tf_op jit(solution)/shard_map/ppermute | solution.py:241
  62.1 0.0 collective-permute-done.3.third
  62.1 0.0 collective-permute-done.4.fourth
  62.1 0.0 copy-done.3
  62.1 1.8 %shard_map.60 = f32[4,2,64,128]{3,2,1,0:T(8,128)} custom-call(f32[4,2,64,128]{3,2,1,0:T(8,128)S(1)} %copy-done.3, f32[4,2,64,128]{3,2,1,0:T(8,128)S(1)} %collective-permute-done.2.second, f32[4,2,64,128]{3,2,1,0:T(8,128)} %collective-permute-done.3.third, f32[4,2,64,128]{3,2,1,0:T(8,128)} %collective-permute-done.4.fourth), custom_call_target="tpu_custom_call" | custom-call | flops 18119393280 | bytes 1048576 | tf_op jit(solution)/shard_map/pallas_call | solution.py:149
  63.9 9.4 %all-to-all-start.1 = ((f32[4,2,64,128]{3,2,1,0:T(8,128)}), f32[4,2,64,128]{3,2,1,0:T(8,128)S(1)}, u32[]{:S(2)}, u32[]{:S(2)}) async-start(f32[4,2,64,128]{3,2,1,0:T(8,128)} %shard_map.60), calls=%async_computation.1 | async-start | bytes 524288 | tf_op jit(solution)/shard_map/all_to_all | solution.py:182
  73.3 0.0 collective-permute-done.6.high
  73.3 0.0 collective-permute-done.5.low
  73.3 0.0 copy-done.1
  73.3 1.6 %shard_map.61 = (f32[4,4,32,128]{3,2,1,0:T(8,128)S(1)}, f32[4,4,32,128]{3,2,1,0:T(8,128)S(1)}) custom-call(s32[1]{0:T(128)} %bitcast.13.place, bf16[32,64,128]{2,1,0:T(8,128)(2,1)S(1)} %collective-permute-done.5.low, bf16[32,64,128]{2,1,0:T(8,128)(2,1)S(1)} %bitcast.31, bf16[32,64,128]{2,1,0:T(8,128)(2,1)S(1)} %collective-permute-done.6.high, ...), custom_call_target="tpu_custom_call" | custom-call | flops 18119393280 | bytes 1683460 | tf_op jit(solution)/shard_map/pallas_call | solution.py:149
  75.0 1.9 %collective-permute-start.7 = (f32[4,4,32,128]{3,2,1,0:T(8,128)S(1)}, f32[4,4,32,128]{3,2,1,0:T(8,128)S(1)}, u32[]{:S(2)}, u32[]{:S(2)}) collective-permute-start(f32[4,4,32,128]{3,2,1,0:T(8,128)S(1)} %get-tuple-element.29), channel_id=1, source_target_pairs={{0,4},{4,0},{8,12},{12,8},{16,20},{20,16},{24,28},{28,24},{1,5},{5... | collective-permute-start | bytes 786440 | tf_op jit(solution)/shard_map/ppermute | solution.py:265
  76.9 0.0 collective-permute-done.11
  77.0 4.5 %collective-permute-start.12 = (f32[448,128]{1,0:T(8,128)S(1)}, f32[448,128]{1,0:T(8,128)S(1)}, u32[]{:S(2)}, u32[]{:S(2)}) collective-permute-start(f32[448,128]{1,0:T(8,128)S(1)} %add.3.near), channel_id=1, source_target_pairs={{0,3},{1,2},{2,1},{3,0},{4,7},{5,6},{6,5},{7,4},{8,11},{9,10},{10,... | collective-permute-start | bytes 688136 | tf_op jit(solution)/shard_map/ppermute | solution.py:267
  81.5 0.0 collective-permute-done.7.came
  81.5 3.4 %collective-permute-start.8 = (f32[4,32,128]{2,1,0:T(8,128)S(1)}, f32[4,32,128]{2,1,0:T(8,128)S(1)}, u32[]{:S(2)}, u32[]{:S(2)}) collective-permute-start(f32[4,32,128]{2,1,0:T(8,128)S(1)} %get-tuple-element.31), channel_id=1, source_target_pairs={{0,16},{4,20},{8,24},{12,28},{16,0},{20,4},{24,8},{28,12},{1,17},{... | collective-permute-start | bytes 196616 | tf_op jit(solution)/shard_map/ppermute | solution.py:274
  84.9 2.7 %collective-permute-start.9 = (f32[4,32,128]{2,1,0:T(8,128)S(1)}, f32[4,32,128]{2,1,0:T(8,128)S(1)}, u32[]{:S(2)}, u32[]{:S(2)}) collective-permute-start(f32[4,32,128]{2,1,0:T(8,128)S(1)} %get-tuple-element.32), channel_id=1, source_target_pairs={{0,8},{4,12},{8,16},{12,20},{16,24},{20,28},{24,0},{28,4},{1,9},{5... | collective-permute-start | bytes 196616 | tf_op jit(solution)/shard_map/ppermute | solution.py:274
  87.5 3.2 %collective-permute-start.10 = (f32[4,32,128]{2,1,0:T(8,128)S(1)}, f32[4,32,128]{2,1,0:T(8,128)S(1)}, u32[]{:S(2)}, u32[]{:S(2)}) collective-permute-start(f32[4,32,128]{2,1,0:T(8,128)S(1)} %get-tuple-element.33), channel_id=1, source_target_pairs={{0,24},{4,28},{8,0},{12,4},{16,8},{20,12},{24,16},{28,20},{1,25},{... | collective-permute-start | bytes 196616 | tf_op jit(solution)/shard_map/ppermute | solution.py:274
  90.7 0.0 collective-permute-done.12.far
  90.8 0.8 shard_map.64
  91.6 0.0 all-to-all-done.1
  91.6 0.6 copy.11
  92.2 0.0 collective-permute-done.8.second
  92.2 0.0 collective-permute-done.9.third
  92.2 2.7 %collective-permute-done.10.fourth = f32[4,32,128]{2,1,0:T(8,128)S(1)} collective-permute-done((f32[4,32,128]{2,1,0:T(8,128)S(1)}, f32[4,32,128]{2,1,0:T(8,128)S(1)}, u32[]{:S(2)}, u32[]{:S(2)}) %collective-permute-start.10) | collective-permute-done | bytes 65568 | tf_op jit(solution)/shard_map/ppermute | solution.py:274
  94.9 0.6 copy.12
  (9 shorter events, 0.1 us)
Async XLA Ops:
  0.6 5.5 %copy-start.4 = (bf16[64,1,2,128]{3,2,1,0:T(2,128)(2,1)S(1)}, bf16[64,1,2,128]{3,2,1,0:T(2,128)(2,1)}, u32[]{:S(2)}) copy-start(bf16[64,1,2,128]{3,2,1,0:T(2,128)(2,1)} %param.5) | copy-start | bytes 98308
  1.4 20.9 %collective-permute-start = (bf16[4,32,128]{2,1,0:T(8,128)(2,1)S(1)}, bf16[4,32,128]{2,1,0:T(8,128)(2,1)S(1)}, u32[]{:S(2)}, u32[]{:S(2)}) collective-permute-start(bf16[4,32,128]{2,1,0:T(8,128)(2,1)S(1)} %bitcast.33), channel_id=1, source_target_pairs={{0,1},{1,2},{2,3},{4,5},{5,6},{6,7},{8,9},{9,10},{10,11},{12,13},{... | collective-permute-start | bytes 98312 | tf_op jit(solution)/shard_map/ppermute | solution.py:163
  4.8 17.5 %collective-permute-start.1 = (bf16[4,32,128]{2,1,0:T(8,128)(2,1)S(1)}, bf16[4,32,128]{2,1,0:T(8,128)(2,1)S(1)}, u32[]{:S(2)}, u32[]{:S(2)}) collective-permute-start(bf16[4,32,128]{2,1,0:T(8,128)(2,1)S(1)} %bitcast.34), channel_id=1, source_target_pairs={{1,0},{2,1},{3,2},{5,4},{6,5},{7,6},{9,8},{10,9},{11,10},{13,12},{... | collective-permute-start | bytes 98312 | tf_op jit(solution)/shard_map/ppermute | solution.py:163
  7.1 43.9 %all-to-all-start = ((bf16[16,2,64,128]{3,2,1,0:T(8,128)(2,1)}), bf16[16,2,64,128]{3,2,1,0:T(8,128)(2,1)S(1)}, u32[]{:S(2)}, u32[]{:S(2)}) async-start(bf16[16,2,64,128]{3,2,1,0:T(8,128)(2,1)} %broadcast_in_dim.2), calls=%async_computation | async-start | bytes 1048576 | tf_op jit(solution)/shard_map/all_to_all | solution.py:182
  22.3 13.6 %copy-start = (bf16[3,3,3,32,64]{4,3,2,1,0:T(8,128)(2,1)S(1)}, bf16[3,3,3,32,64]{4,3,2,1,0:T(8,128)(2,1)}, u32[]{:S(2)}) copy-start(bf16[3,3,3,32,64]{4,3,2,1,0:T(8,128)(2,1)} %weights.3) | copy-start | bytes 331780
  38.2 0.7 copy-start.2
  38.9 19.2 %collective-permute-start.2 = (f32[4,2,64,128]{3,2,1,0:T(8,128)}, f32[4,2,64,128]{3,2,1,0:T(8,128)S(1)}, u32[]{:S(2)}, u32[]{:S(2)}) collective-permute-start(f32[4,2,64,128]{3,2,1,0:T(8,128)} %get-tuple-element.23), channel_id=1, source_target_pairs={{0,32},{32,64},{64,96},{96,128},{128,160},{160,192},{192,224},{224... | collective-permute-start | bytes 786440 | tf_op jit(solution)/shard_map/ppermute | solution.py:168
  42.7 19.3 %collective-permute-start.3 = (f32[4,2,64,128]{3,2,1,0:T(8,128)S(1)}, f32[4,2,64,128]{3,2,1,0:T(8,128)}, u32[]{:S(2)}, u32[]{:S(2)}) collective-permute-start(f32[4,2,64,128]{3,2,1,0:T(8,128)S(1)} %get-tuple-element.24), channel_id=1, source_target_pairs={{0,480},{32,0},{64,32},{96,64},{128,96},{160,128},{192,160},{224,1... | collective-permute-start | bytes 786440 | tf_op jit(solution)/shard_map/ppermute | solution.py:168
  46.0 16.1 %collective-permute-start.4 = (f32[4,2,64,128]{3,2,1,0:T(8,128)S(1)}, f32[4,2,64,128]{3,2,1,0:T(8,128)}, u32[]{:S(2)}, u32[]{:S(2)}) collective-permute-start(f32[4,2,64,128]{3,2,1,0:T(8,128)S(1)} %get-tuple-element.25), channel_id=1, source_target_pairs={{0,64},{4,452},{8,72},{12,460},{16,80},{20,468},{24,88},{28,476},{... | collective-permute-start | bytes 786440 | tf_op jit(solution)/shard_map/ppermute | solution.py:178
  51.0 11.1 %copy-start.3 = (f32[4,2,64,128]{3,2,1,0:T(8,128)S(1)}, f32[4,2,64,128]{3,2,1,0:T(8,128)}, u32[]{:S(2)}) copy-start(f32[4,2,64,128]{3,2,1,0:T(8,128)} %copy-done.2) | copy-start | bytes 786436
  51.0 22.4 %collective-permute-start.6 = (bf16[32,64,128]{2,1,0:T(8,128)(2,1)S(1)}, bf16[32,64,128]{2,1,0:T(8,128)(2,1)S(1)}, u32[]{:S(2)}, u32[]{:S(2)}) collective-permute-start(bf16[32,64,128]{2,1,0:T(8,128)(2,1)S(1)} %bitcast.28), channel_id=1, source_target_pairs={{1,0},{2,1},{3,2},{5,4},{6,5},{7,6},{9,8},{10,9},{11,10},{13,12},{... | collective-permute-start | bytes 1572872 | tf_op jit(solution)/shard_map/ppermute | solution.py:163
  52.4 21.0 %collective-permute-start.5 = (bf16[32,64,128]{2,1,0:T(8,128)(2,1)S(1)}, bf16[32,64,128]{2,1,0:T(8,128)(2,1)S(1)}, u32[]{:S(2)}, u32[]{:S(2)}) collective-permute-start(bf16[32,64,128]{2,1,0:T(8,128)(2,1)S(1)} %bitcast.29), channel_id=1, source_target_pairs={{0,1},{1,2},{2,3},{4,5},{5,6},{6,7},{8,9},{9,10},{10,11},{12,13},{... | collective-permute-start | bytes 1572872 | tf_op jit(solution)/shard_map/ppermute | solution.py:163
  58.2 18.8 %collective-permute-start.11 = (f32[448,128]{1,0:T(8,128)S(1)}, f32[448,128]{1,0:T(8,128)S(1)}, u32[]{:S(2)}, u32[]{:S(2)}) collective-permute-start(f32[448,128]{1,0:T(8,128)S(1)} %shard_map.59), channel_id=1, source_target_pairs={{0,1},{1,0},{2,3},{3,2},{4,5},{5,4},{6,7},{7,6},{8,9},{9,8},{10,11... | collective-permute-start | bytes 688136 | tf_op jit(solution)/shard_map/ppermute | solution.py:241
  63.9 9.5 %copy-start.1 = (bf16[3,3,3,32,64]{4,3,2,1,0:T(8,128)(2,1)S(1)}, bf16[3,3,3,32,64]{4,3,2,1,0:T(8,128)(2,1)}, u32[]{:S(2)}) copy-start(bf16[3,3,3,32,64]{4,3,2,1,0:T(8,128)(2,1)} %weights.3) | copy-start | bytes 331780
  63.9 27.7 %all-to-all-start.1 = ((f32[4,2,64,128]{3,2,1,0:T(8,128)}), f32[4,2,64,128]{3,2,1,0:T(8,128)S(1)}, u32[]{:S(2)}, u32[]{:S(2)}) async-start(f32[4,2,64,128]{3,2,1,0:T(8,128)} %shard_map.60), calls=%async_computation.1 | async-start | bytes 524288 | tf_op jit(solution)/shard_map/all_to_all | solution.py:182
  75.0 6.5 %collective-permute-start.7 = (f32[4,4,32,128]{3,2,1,0:T(8,128)S(1)}, f32[4,4,32,128]{3,2,1,0:T(8,128)S(1)}, u32[]{:S(2)}, u32[]{:S(2)}) collective-permute-start(f32[4,4,32,128]{3,2,1,0:T(8,128)S(1)} %get-tuple-element.29), channel_id=1, source_target_pairs={{0,4},{4,0},{8,12},{12,8},{16,20},{20,16},{24,28},{28,24},{1,5},{5... | collective-permute-start | bytes 786440 | tf_op jit(solution)/shard_map/ppermute | solution.py:265
  77.0 13.8 %collective-permute-start.12 = (f32[448,128]{1,0:T(8,128)S(1)}, f32[448,128]{1,0:T(8,128)S(1)}, u32[]{:S(2)}, u32[]{:S(2)}) collective-permute-start(f32[448,128]{1,0:T(8,128)S(1)} %add.3.near), channel_id=1, source_target_pairs={{0,3},{1,2},{2,1},{3,0},{4,7},{5,6},{6,5},{7,4},{8,11},{9,10},{10,... | collective-permute-start | bytes 688136 | tf_op jit(solution)/shard_map/ppermute | solution.py:267
  81.5 10.7 %collective-permute-start.8 = (f32[4,32,128]{2,1,0:T(8,128)S(1)}, f32[4,32,128]{2,1,0:T(8,128)S(1)}, u32[]{:S(2)}, u32[]{:S(2)}) collective-permute-start(f32[4,32,128]{2,1,0:T(8,128)S(1)} %get-tuple-element.31), channel_id=1, source_target_pairs={{0,16},{4,20},{8,24},{12,28},{16,0},{20,4},{24,8},{28,12},{1,17},{... | collective-permute-start | bytes 196616 | tf_op jit(solution)/shard_map/ppermute | solution.py:274
  84.9 7.4 %collective-permute-start.9 = (f32[4,32,128]{2,1,0:T(8,128)S(1)}, f32[4,32,128]{2,1,0:T(8,128)S(1)}, u32[]{:S(2)}, u32[]{:S(2)}) collective-permute-start(f32[4,32,128]{2,1,0:T(8,128)S(1)} %get-tuple-element.32), channel_id=1, source_target_pairs={{0,8},{4,12},{8,16},{12,20},{16,24},{20,28},{24,0},{28,4},{1,9},{5... | collective-permute-start | bytes 196616 | tf_op jit(solution)/shard_map/ppermute | solution.py:274
  87.5 7.4 %collective-permute-start.10 = (f32[4,32,128]{2,1,0:T(8,128)S(1)}, f32[4,32,128]{2,1,0:T(8,128)S(1)}, u32[]{:S(2)}, u32[]{:S(2)}) collective-permute-start(f32[4,32,128]{2,1,0:T(8,128)S(1)} %get-tuple-element.33), channel_id=1, source_target_pairs={{0,24},{4,28},{8,0},{12,4},{16,8},{20,12},{24,16},{28,20},{1,25},{... | collective-permute-start | bytes 196616 | tf_op jit(solution)/shard_map/ppermute | solution.py:274
